TPU v7x, 32 devices: a whole 2x2x4 slice. The times are simulated.
32 devices in a mesh: dp: 16 (over z, y, core), head: 2 (over x).
Axes of the slice: x: 2, y: 2, z: 4, core: 2. Of those that a mesh axis runs over, the one named last changes fastest.
Arguments:
- segment: bfloat16 [32, 512, 1024], P(('dp', 'head')), may hold values from -6 to 6
- memory: bfloat16 [32, 512, 1024], P('dp'), may hold values from -6 to 6
- compressed: bfloat16 [32, 512, 1024], P('dp'), may hold values from -6 to 6
- doc_lengths: int32 [32, 4], P('dp'), may hold values from 1 to 256, 512 in all within a row
- memory_valid: int32 [32], P('dp'), may hold values from 1 to 1024
- query_weight: bfloat16 [1024, 1024], P('dp', 'head'), may hold values from -0.1875 to 0.1875
- key_weight: bfloat16 [1024, 1024], P('dp', 'head'), may hold values from -0.1875 to 0.1875
- value_weight: bfloat16 [1024, 1024], P('dp', 'head'), may hold values from -0.1875 to 0.1875
- position_weight: bfloat16 [1024, 1024], P('dp', 'head'), may hold values from -0.1875 to 0.1875
- content_bias: bfloat16 [8, 128], P('head', 'dp'), may hold values from -3 to 3
- position_bias: bfloat16 [8, 128], P('head', 'dp'), may hold values from -3 to 3
- output_weight: bfloat16 [1024, 1024], P(('dp', 'head')), may hold values from -0.75 to 0.75
- up_weight: bfloat16 [1024, 4096], P(('dp', 'head')), may hold values from -0.1875 to 0.1875
- down_weight: bfloat16 [4096, 1024], P(('dp', 'head')), may hold values from -0.09375 to 0.09375
- compress_weight: bfloat16 [3072, 1024], P(('dp', 'head')), may hold values from -0.109375 to 0.109375
- norm_gain: bfloat16 [1024], P(('dp', 'head')), may hold values from 0.099609375 to 1.8984375
- norm_shift: bfloat16 [1024], P(('dp', 'head')), may hold values from -3 to 3
- post_gain: bfloat16 [1024], P(('dp', 'head')), may hold values from 0.099609375 to 1.8984375
- post_shift: bfloat16 [1024], P(('dp', 'head')), may hold values from -3 to 3
- cotangent: bfloat16 [32, 512, 1024], P(('dp', 'head')), may hold values from -6 to 6
- compress_cotangent: bfloat16 [32, 170, 1024], P(('dp', 'head')), may hold values from -6 to 6
Outputs:
- output: bfloat16 [32, 512, 1024], P(('dp', 'head'))
- new_compressed: bfloat16 [32, 170, 1024], P(('dp', 'head'))
- segment_gradient: bfloat16 [32, 512, 1024], P(('dp', 'head'))
- query_gradient: float32 [1024, 1024], P('dp', 'head')
- key_gradient: float32 [1024, 1024], P('dp', 'head')
- value_gradient: float32 [1024, 1024], P('dp', 'head')
- position_gradient: float32 [1024, 1024], P('dp', 'head')
- content_bias_gradient: float32 [8, 128], P('head', 'dp')
- position_bias_gradient: float32 [8, 128], P('head', 'dp')
- output_gradient: float32 [1024, 1024], P(('dp', 'head'))
- up_gradient: float32 [1024, 4096], P(('dp', 'head'))
- down_gradient: float32 [4096, 1024], P(('dp', 'head'))
- compress_gradient: float32 [3072, 1024], P(('dp', 'head'))
- norm_gain_gradient: float32 [1024], P(('dp', 'head'))
- norm_shift_gradient: float32 [1024], P(('dp', 'head'))
- post_gain_gradient: float32 [1024], P(('dp', 'head'))
- post_shift_gradient: float32 [1024], P(('dp', 'head'))
Inputs may be any that keep to these rules, and one draw needn't show every extreme that they name: `doc_lengths`: each row gives the lengths, in order, of the 4 documents packed into a segment of 512 tokens; the first continues from the memory. `memory_valid`: the first document sees this many of the most recent rows of compressed then memory.
All inputs are finite; a program needn't handle non-finite values.
Results may differ from a plain program's by a relative error of at most 0.028.
Values may be sent and summed in bfloat16 or wider, within the bound.
A program may use at most 384 MiB of HBM per device.

v0:
```python
import math

import jax
import jax.numpy as jnp
from jax import lax
from jax.sharding import PartitionSpec as P


def layer_norm(values, gain, shift):
    row_mean = jnp.mean(values, axis=-1, keepdims=True)
    centred = values - row_mean
    row_variance = jnp.mean(centred * centred, axis=-1, keepdims=True)
    return centred * lax.rsqrt(row_variance + 1e-05) * gain + shift


def position_table(context, model_width):
    distance = jnp.arange(context, dtype=jnp.float32)[:, None]
    frequency = jnp.exp(
        jnp.arange(model_width // 2, dtype=jnp.float32) * (-2.0 * math.log(10000.0) / model_width)
    )
    phases = distance * frequency[None, :]
    return jnp.concatenate([jnp.sin(phases), jnp.cos(phases)], axis=1)


def visible(lengths, valid_len, seg_len, past_rows):
    doc_ends = jnp.cumsum(lengths)
    position = jnp.arange(seg_len, dtype=jnp.int32)
    doc_index = jnp.sum((position[:, None] >= doc_ends[None, :]).astype(jnp.int32), axis=1)
    same_doc = (doc_index[:, None] == doc_index[None, :]) & (position[None, :] <= position[:, None])
    slots = jnp.arange(past_rows, dtype=jnp.int32)
    mem_seen = (doc_index[:, None] == 0) & (slots[None, :] >= past_rows - valid_len)
    return jnp.concatenate([mem_seen, same_doc], axis=1)


def skew_rows(flipped):
    head_count, seg_len, context = flipped.shape
    padded = jnp.pad(flipped, ((0, 0), (0, 0), (0, seg_len)))
    flattened = padded.reshape(head_count, seg_len * (context + seg_len))
    selected = lax.slice_in_dim(
        flattened, seg_len - 1, seg_len - 1 + seg_len * (context + seg_len - 1), axis=1
    )
    return selected.reshape(head_count, seg_len, context + seg_len - 1)[:, :, :context]


def attention_weights(query_content, query_place, keys_proj, place_keys, seen_mask, head_count):
    seg_len = query_content.shape[0]
    context = keys_proj.shape[0]
    head_size = keys_proj.shape[1] // head_count
    content_heads = query_content.reshape(seg_len, head_count, head_size)
    position_head_rows = query_place.reshape(seg_len, head_count, head_size)
    key_heads = keys_proj.reshape(context, head_count, head_size)
    position_key_heads = place_keys.reshape(context, head_count, head_size)
    content = jnp.einsum(
        "ihd,jhd->hij", content_heads, key_heads, preferred_element_type=jnp.float32
    )
    flipped = jnp.einsum(
        "fuw,buw->ufb", position_head_rows, position_key_heads, preferred_element_type=jnp.float32
    )
    scores = (content + skew_rows(flipped)) * (1.0 / math.sqrt(head_size))
    scores = jnp.where(seen_mask[None], scores, -1e30)
    row_max = jnp.max(scores, axis=2, keepdims=True)
    expo_vals = jnp.exp(scores - row_max)
    return expo_vals / jnp.sum(expo_vals, axis=2, keepdims=True)


def body(
    segment,
    memory,
    compressed,
    doc_lengths,
    memory_valid,
    query_weight,
    key_weight,
    value_weight,
    position_weight,
    content_bias,
    position_bias,
    output_weight,
    up_weight,
    down_weight,
    compress_weight,
    norm_gain,
    norm_shift,
    post_gain,
    post_shift,
    cotangent,
    compress_cotangent,
):
    query_mat, key_mat, value_mat, place_mat, content_vec, place_vec = (
        lax.all_gather(query_weight, "dp", axis=0, tiled=True),
        lax.all_gather(key_weight, "dp", axis=0, tiled=True),
        lax.all_gather(value_weight, "dp", axis=0, tiled=True),
        lax.all_gather(position_weight, "dp", axis=0, tiled=True),
        lax.all_gather(content_bias, "dp", axis=1, tiled=True),
        lax.all_gather(position_bias, "dp", axis=1, tiled=True),
    )
    out_mat, up_mat, down_mat, comp_mat, gain_one, shift_one, gain_two, shift_two = (
        lax.all_gather(output_weight, ("dp", "head"), axis=0, tiled=True),
        lax.all_gather(up_weight, ("dp", "head"), axis=0, tiled=True),
        lax.all_gather(down_weight, ("dp", "head"), axis=0, tiled=True),
        lax.all_gather(compress_weight, ("dp", "head"), axis=0, tiled=True),
        lax.all_gather(norm_gain, ("dp", "head"), axis=0, tiled=True),
        lax.all_gather(norm_shift, ("dp", "head"), axis=0, tiled=True),
        lax.all_gather(post_gain, ("dp", "head"), axis=0, tiled=True),
        lax.all_gather(post_shift, ("dp", "head"), axis=0, tiled=True),
    )
    row_pairs = lax.all_gather(segment, "head", axis=0, tiled=True)
    seg_len = segment.shape[1]
    model_width = segment.shape[2]
    own_count = segment.shape[0]
    past_rows = memory.shape[1] + compressed.shape[1]
    context = past_rows + seg_len
    head_count = content_vec.shape[0]
    head_size = content_vec.shape[1]
    half_width = query_mat.shape[1]
    head_pos = lax.axis_index("head")
    score_scale = 1.0 / math.sqrt(head_size)
    gain_one_f = gain_one.astype(jnp.float32)
    shift_one_f = shift_one.astype(jnp.float32)
    gain_two_f = gain_two.astype(jnp.float32)
    shift_two_f = shift_two.astype(jnp.float32)
    content_flat = content_vec.astype(jnp.float32).reshape(-1)
    place_flat = place_vec.astype(jnp.float32).reshape(-1)
    table_rev = position_table(context, model_width).astype(jnp.bfloat16)[::-1]
    place_keys = jnp.dot(table_rev, place_mat, preferred_element_type=jnp.float32).astype(
        jnp.bfloat16
    )

    def forward_one(element):
        row_block, memory_rows, compressed_rows, lengths, valid_len = element
        context_in = jnp.concatenate([compressed_rows, memory_rows, row_block], axis=0).astype(
            jnp.float32
        )
        normed = layer_norm(context_in, gain_one_f, shift_one_f).astype(jnp.bfloat16)
        queries = jnp.dot(normed[past_rows:], query_mat, preferred_element_type=jnp.float32)
        keys_proj = jnp.dot(normed, key_mat, preferred_element_type=jnp.float32).astype(
            jnp.bfloat16
        )
        values_proj = jnp.dot(normed, value_mat, preferred_element_type=jnp.float32).astype(
            jnp.bfloat16
        )
        query_content = (queries + content_flat).astype(jnp.bfloat16)
        query_place = (queries + place_flat).astype(jnp.bfloat16)
        seen_mask = visible(lengths, valid_len, seg_len, past_rows)
        attn_low = attention_weights(
            query_content, query_place, keys_proj, place_keys, seen_mask, head_count
        ).astype(jnp.bfloat16)
        value_heads = values_proj.reshape(context, head_count, head_size)
        attended = jnp.einsum(
            "hij,jhd->ihd", attn_low, value_heads, preferred_element_type=jnp.float32
        )
        return (
            normed,
            query_content,
            query_place,
            keys_proj,
            values_proj,
            attended.reshape(seg_len, half_width).astype(jnp.bfloat16),
        )

    normed_all, content_all, place_q_all, keys_all, values_all, attended_all = lax.map(
        forward_one, (row_pairs, memory, compressed, doc_lengths, memory_valid)
    )
    mixed = lax.all_to_all(attended_all, "head", split_axis=0, concat_axis=2, tiled=True)
    segment_f = segment.astype(jnp.float32)
    residual = segment_f + jnp.einsum(
        "sic,cd->sid", mixed, out_mat, preferred_element_type=jnp.float32
    )
    normed_two = layer_norm(residual, gain_two_f, shift_two_f).astype(jnp.bfloat16)
    hidden_pre = jnp.einsum("sid,df->sif", normed_two, up_mat, preferred_element_type=jnp.float32)
    hidden_act = jax.nn.gelu(hidden_pre).astype(jnp.bfloat16)
    branch_out = jnp.einsum("sif,fd->sid", hidden_act, down_mat, preferred_element_type=jnp.float32)
    result = (residual + branch_out).astype(jnp.bfloat16)
    new_count = compress_cotangent.shape[1]
    own_start = head_pos * own_count
    own_memory = lax.dynamic_slice_in_dim(memory, own_start, own_count, 0)
    windows = own_memory[:, : 3 * new_count].reshape(own_count, new_count, 3 * model_width)
    made = jnp.einsum("sca,ab->scb", windows, comp_mat, preferred_element_type=jnp.float32).astype(
        jnp.bfloat16
    )
    down_grad = jnp.einsum("sif,sid->fd", hidden_act, cotangent, preferred_element_type=jnp.float32)
    act_grad = jnp.einsum(
        "sid,fd->sif", cotangent, down_mat, preferred_element_type=jnp.float32
    ).astype(jnp.bfloat16)
    hidden_vals, gelu_back = jax.vjp(jax.nn.gelu, hidden_pre)
    pre_grad = gelu_back(act_grad.astype(jnp.float32))[0].astype(jnp.bfloat16)
    up_grad = jnp.einsum("sid,sif->df", normed_two, pre_grad, preferred_element_type=jnp.float32)
    input_terms = jnp.einsum("sif,df->sid", pre_grad, up_mat, preferred_element_type=jnp.float32)
    norm_vals, post_back = jax.vjp(layer_norm, residual, gain_two_f, shift_two_f)
    residual_part, gain_two_grad, shift_two_grad = post_back(input_terms)
    residual_grad = cotangent.astype(jnp.float32) + residual_part
    branch_grad = residual_grad.astype(jnp.bfloat16)
    out_grad = jnp.einsum("sic,sid->cd", mixed, branch_grad, preferred_element_type=jnp.float32)
    mixed_grad = jnp.einsum(
        "sid,cd->sic", branch_grad, out_mat, preferred_element_type=jnp.float32
    ).astype(jnp.bfloat16)
    attended_grads = lax.all_to_all(mixed_grad, "head", split_axis=2, concat_axis=0, tiled=True)

    def backward_one(element):
        (
            row_block,
            memory_rows,
            compressed_rows,
            lengths,
            valid_len,
            normed,
            query_content,
            query_place,
            keys_proj,
            values_proj,
            attended_grad,
        ) = element
        context_in = jnp.concatenate([compressed_rows, memory_rows, row_block], axis=0).astype(
            jnp.float32
        )
        seen_mask = visible(lengths, valid_len, seg_len, past_rows)
        attn_full = attention_weights(
            query_content, query_place, keys_proj, place_keys, seen_mask, head_count
        )
        attn_low = attn_full.astype(jnp.bfloat16)
        grad_heads = attended_grad.reshape(seg_len, head_count, head_size)
        value_heads = values_proj.reshape(context, head_count, head_size)
        key_heads = keys_proj.reshape(context, head_count, head_size)
        content_heads = query_content.reshape(seg_len, head_count, head_size)
        position_head_rows = query_place.reshape(seg_len, head_count, head_size)
        position_key_heads = place_keys.reshape(context, head_count, head_size)
        values_grad = (
            jnp.einsum("hij,ihd->jhd", attn_low, grad_heads, preferred_element_type=jnp.float32)
            .reshape(context, half_width)
            .astype(jnp.bfloat16)
        )
        weights_grad = jnp.einsum(
            "ihd,jhd->hij", grad_heads, value_heads, preferred_element_type=jnp.float32
        )
        scores_grad = attn_full * (
            weights_grad - jnp.sum(weights_grad * attn_full, axis=2, keepdims=True)
        )
        scores_grad = (jnp.where(seen_mask[None], scores_grad, 0.0) * score_scale).astype(
            jnp.bfloat16
        )
        content_grad = (
            jnp.einsum("hij,jhd->ihd", scores_grad, key_heads, preferred_element_type=jnp.float32)
            .reshape(seg_len, half_width)
            .astype(jnp.bfloat16)
        )
        keys_grad = (
            jnp.einsum(
                "hij,ihd->jhd", scores_grad, content_heads, preferred_element_type=jnp.float32
            )
            .reshape(context, half_width)
            .astype(jnp.bfloat16)
        )
        skewed_values, skew_back = jax.vjp(
            skew_rows, jnp.zeros((head_count, seg_len, context), jnp.float32)
        )
        reversed_gradient = skew_back(scores_grad.astype(jnp.float32))[0].astype(jnp.bfloat16)
        place_grad = (
            jnp.einsum(
                "zaw,wzc->azc",
                reversed_gradient,
                position_key_heads,
                preferred_element_type=jnp.float32,
            )
            .reshape(seg_len, half_width)
            .astype(jnp.bfloat16)
        )
        place_keys_grad = (
            jnp.einsum(
                "kgl,gkf->lkf",
                reversed_gradient,
                position_head_rows,
                preferred_element_type=jnp.float32,
            )
            .reshape(context, half_width)
            .astype(jnp.bfloat16)
        )
        content_f = content_grad.astype(jnp.float32)
        place_f = place_grad.astype(jnp.float32)
        queries_grad = (content_f + place_f).astype(jnp.bfloat16)
        normed_grad = jnp.einsum(
            "jc,dc->jd", keys_grad, key_mat, preferred_element_type=jnp.float32
        )
        normed_grad = normed_grad + jnp.einsum(
            "jc,dc->jd", values_grad, value_mat, preferred_element_type=jnp.float32
        )
        normed_grad = normed_grad.at[past_rows:].add(
            jnp.einsum("ic,dc->id", queries_grad, query_mat, preferred_element_type=jnp.float32)
        )
        norm_out, norm_back = jax.vjp(layer_norm, context_in, gain_one_f, shift_one_f)
        context_grad, gain_part, shift_part = norm_back(normed_grad)
        return (
            context_grad[past_rows:],
            gain_part,
            shift_part,
            queries_grad,
            keys_grad,
            values_grad,
            place_keys_grad,
            jnp.sum(content_f, axis=0),
            jnp.sum(place_f, axis=0),
        )

    (
        rows_grad,
        gain_parts,
        shift_parts,
        queries_grads,
        keys_grads,
        values_grads,
        place_grads,
        content_totals,
        place_sums,
    ) = lax.map(
        backward_one,
        (
            row_pairs,
            memory,
            compressed,
            doc_lengths,
            memory_valid,
            normed_all,
            content_all,
            place_q_all,
            keys_all,
            values_all,
            attended_grads,
        ),
    )
    query_grad = jnp.einsum(
        "sid,sic->dc", normed_all[:, past_rows:], queries_grads, preferred_element_type=jnp.float32
    )
    key_grad = jnp.einsum("smd,smc->dc", normed_all, keys_grads, preferred_element_type=jnp.float32)
    value_grad = jnp.einsum(
        "smd,smc->dc", normed_all, values_grads, preferred_element_type=jnp.float32
    )
    place_weight_grad = jnp.einsum(
        "md,smc->dc", table_rev, place_grads, preferred_element_type=jnp.float32
    )
    content_bias_grad = jnp.sum(content_totals, axis=0).reshape(head_count, head_size)
    place_bias_grad = jnp.sum(place_sums, axis=0).reshape(head_count, head_size)
    gain_one_grad = jnp.sum(gain_parts, axis=0)
    shift_one_grad = jnp.sum(shift_parts, axis=0)
    gain_two_sum = jnp.sum(gain_two_grad.reshape(-1, model_width), axis=0)
    shift_two_sum = jnp.sum(shift_two_grad.reshape(-1, model_width), axis=0)
    input_part = lax.psum_scatter(
        rows_grad.astype(jnp.bfloat16), "head", scatter_dimension=0, tiled=True
    ).astype(jnp.float32)
    segment_grad = (residual_grad + input_part).astype(jnp.bfloat16)
    comp_grad = jnp.einsum(
        "sca,scb->ab", windows, compress_cotangent, preferred_element_type=jnp.float32
    )
    query_shard, key_shard, value_shard, place_shard, content_shard, place_bias_shard = (
        lax.psum_scatter(query_grad, "dp", scatter_dimension=0, tiled=True),
        lax.psum_scatter(key_grad, "dp", scatter_dimension=0, tiled=True),
        lax.psum_scatter(value_grad, "dp", scatter_dimension=0, tiled=True),
        lax.psum_scatter(place_weight_grad, "dp", scatter_dimension=0, tiled=True),
        lax.psum_scatter(content_bias_grad, "dp", scatter_dimension=1, tiled=True),
        lax.psum_scatter(place_bias_grad, "dp", scatter_dimension=1, tiled=True),
    )
    (
        out_shard,
        up_shard,
        down_shard,
        comp_shard,
        gain_one_shard,
        shift_one_shard,
        gain_two_shard,
        shift_two_shard,
    ) = (
        lax.psum_scatter(out_grad, ("dp", "head"), scatter_dimension=0, tiled=True),
        lax.psum_scatter(up_grad, ("dp", "head"), scatter_dimension=0, tiled=True),
        lax.psum_scatter(down_grad, ("dp", "head"), scatter_dimension=0, tiled=True),
        lax.psum_scatter(comp_grad, ("dp", "head"), scatter_dimension=0, tiled=True),
        lax.psum_scatter(gain_one_grad, ("dp", "head"), scatter_dimension=0, tiled=True),
        lax.psum_scatter(shift_one_grad, ("dp", "head"), scatter_dimension=0, tiled=True),
        lax.psum_scatter(gain_two_sum, ("dp", "head"), scatter_dimension=0, tiled=True),
        lax.psum_scatter(shift_two_sum, ("dp", "head"), scatter_dimension=0, tiled=True),
    )
    return (
        result,
        made,
        segment_grad,
        query_shard,
        key_shard,
        value_shard,
        place_shard,
        content_shard,
        place_bias_shard,
        out_shard,
        up_shard,
        down_shard,
        comp_shard,
        gain_one_shard,
        shift_one_shard,
        gain_two_shard,
        shift_two_shard,
    )


def solution(mesh):
    return jax.shard_map(
        body,
        mesh=mesh,
        in_specs=(
            P(("dp", "head"), None, None),
            P("dp", None, None),
            P("dp", None, None),
            P("dp", None),
            P("dp"),
            P("dp", "head"),
            P("dp", "head"),
            P("dp", "head"),
            P("dp", "head"),
            P("head", "dp"),
            P("head", "dp"),
            P(("dp", "head"), None),
            P(("dp", "head"), None),
            P(("dp", "head"), None),
            P(("dp", "head"), None),
            P(("dp", "head")),
            P(("dp", "head")),
            P(("dp", "head")),
            P(("dp", "head")),
            P(("dp", "head"), None, None),
            P(("dp", "head"), None, None),
        ),
        out_specs=(
            P(("dp", "head"), None, None),
            P(("dp", "head"), None, None),
            P(("dp", "head"), None, None),
            P("dp", "head"),
            P("dp", "head"),
            P("dp", "head"),
            P("dp", "head"),
            P("head", "dp"),
            P("head", "dp"),
            P(("dp", "head"), None),
            P(("dp", "head"), None),
            P(("dp", "head"), None),
            P(("dp", "head"), None),
            P(("dp", "head")),
            P(("dp", "head")),
            P(("dp", "head")),
            P(("dp", "head")),
        ),
        check_vma=False,
    )
```

profile of v0, /device:TPU:0, one launch (start us, length us, event | category | flops | bytes accessed | tf_op | source)
XLA Modules:
  0.0 2627.9 jit_solution(10100338547050306222)
XLA Ops:
  16.1 42.2 %all-reduce.16 = (bf16[1024]{0:T(1024)(128)(2,1)S(1)}, bf16[1024]{0:T(1024)(128)(2,1)S(1)}, bf16[1024]{0:T(1024)(128)(2,1)}, bf16[1024]{0:T(1024)(128)(2,1)}) all-reduce(bf16[1024]{0:T(1024)(128)(2,1)S(1)} %dynamic-update-slice.6, bf16[1024]{0:T(1024)(128)(2,1)S(1)} %dynamic-update-slice.7, ...), channel_id=1, replica_groups=mesh['dp'=16,'head'=2] {'dp','head'}, use_global_device_ids=true, to_apply=%add.4 | all-reduce | flops 4096 | bytes 16384
  58.3 21.6 all-gather
  80.1 17.7 all-gather.1
  110.4 30.7 %rev.3 = bf16[1536,1024]{1,0:T(8,128)(2,1)} reverse(bf16[1536,1024]{1,0:T(8,128)(2,1)S(1)} %pad_maximum_fusion.2), dimensions={0} | reverse | bytes 6291456 | tf_op jit(solution)/shard_map/rev | solution.py:124
  146.3 21.7 all-gather.18.cloned.1.call-done
  168.0 33.4 %all-gather.12.cloned.1.call-done = bf16[2,512,1024]{2,1,0:T(8,128)(2,1)} async-done(((bf16[1,512,1024]{2,1,0:T(8,128)(2,1)}), bf16[2,512,1024]{2,1,0:T(8,128)(2,1)}) %all-gather.12.cloned.1.call-update) | async-done | bytes 2097168 | tf_op jit(solution)/shard_map/all_gather | solution.py:107
  208.4 387.8 %while.51 = (s32[]{:T(128)}, bf16[2,1536,1024]{2,1,0:T(8,128)(2,1)}, bf16[2,512,512]{1,2,0:T(8,128)(2,1)}, bf16[2,512,512]{1,2,0:T(8,128)(2,1)}, bf16[2,1536,512...) while((s32[]{:T(128)}, ...), condition=%wide.region_7.8_spmd, body=%wide.region_0.7_spmd.sunk | while | flops 6263944704 | bytes 400625280 | solution.py:161
  255.7 19.0 copy.195
  286.1 48.4 %reshape.786 = f32[4192256]{0:T(1024)} reshape(f32[4,1048064]{1,0:T(4,128)} %slice.115) | data formatting | bytes 33538048 | tf_op jit(solution)/shard_map/while
  334.6 25.4 reshape.787
  447.8 19.0 copy.195
  478.1 47.2 %reshape.786 = f32[4192256]{0:T(1024)} reshape(f32[4,1048064]{1,0:T(4,128)} %slice.115) | data formatting | bytes 33538048 | tf_op jit(solution)/shard_map/while
  525.3 25.1 reshape.787
  697.3 605.7 %while.52 = (s32[]{:T(128)}, bf16[2,512,1024]{2,1,0:T(8,128)(2,1)}, f32[2,1024]{1,0:T(2,128)}, f32[2,1024]{1,0:T(2,128)}, bf16[2,512,512]{1,2,0:T(8,128)(2,1)}, ...) while((s32[]{:T(128)}, bf16[2,512,1024]{2,1,0:T(8,128)(2,1)}, ...), condition=%wide.region_26.27_spmd, body=%wide.region_12.26_spmd.sunk | while | flops 11133542400 | bytes 634468096 | solution.py:313
  726.8 19.0 copy.196
  757.3 47.2 %reshape.788 = f32[4192256]{0:T(1024)} reshape(f32[4,1048064]{1,0:T(4,128)} %slice.119) | data formatting | bytes 33538048 | tf_op jit(solution)/shard_map/while
  804.6 24.8 reshape.789
  854.8 17.0 multiply_convert_fusion.5
  908.7 16.3 reshape.790
  1025.4 19.0 copy.196
  1056.0 47.3 %reshape.788 = f32[4192256]{0:T(1024)} reshape(f32[4,1048064]{1,0:T(4,128)} %slice.119) | data formatting | bytes 33538048 | tf_op jit(solution)/shard_map/while
  1103.4 24.8 reshape.789
  1153.6 17.0 multiply_convert_fusion.5
  1413.5 41.0 %all-reduce.14 = (f32[1024]{0:T(1024)S(1)}, f32[1024]{0:T(1024)S(1)}, f32[1024]{0:T(1024)S(1)}, f32[1024]{0:T(1024)S(1)}) all-reduce(f32[1024]{0:T(1024)S(1)} %reduce_sum.328, f32[1024]{0:T(1024)S(1)} %reduce_sum.329, f32[1024]{0:T(1024)S(1)} %copy-done.72, ...), channel_id=13, replica_groups=mesh['dp'=16,'head'=2] {'dp','head'}, use_global_device_ids=true, to_apply=%region_42.43.clone | all-reduce | flops 4096 | bytes 32768
  1456.8 32.3 %all-reduce.15 = (f32[4,128]{1,0:T(4,128)S(1)}, f32[4,128]{1,0:T(4,128)S(1)}) all-reduce(f32[4,128]{1,0:T(4,128)S(1)} %bitcast.435, f32[4,128]{1,0:T(4,128)S(1)} %bitcast.436), channel_id=7, replica_groups=mesh['dp'=16,'head'=2] {'dp'}, use_global_device_ids=true, to_apply=%region_34.35.clone | all-reduce | flops 1024 | bytes 8192
  1498.5 64.9 %reduce-scatter.14.cloned.1.call-done = f32[64,512]{1,0:T(8,128)} async-done(((f32[1024,512]{1,0:T(8,128)}), f32[64,512]{1,0:T(8,128)}) %reduce-scatter.14.cloned.1.call-update) | async-done | bytes 131088 | tf_op jit(solution)/shard_map/reduce_scatter | solution.py:353
  1563.3 65.3 %reduce-scatter.16.cloned.1.call-done = f32[64,512]{1,0:T(8,128)} async-done(((f32[1024,512]{1,0:T(8,128)}), f32[64,512]{1,0:T(8,128)}) %reduce-scatter.16.cloned.1.call-update) | async-done | bytes 131088 | tf_op jit(solution)/shard_map/reduce_scatter | solution.py:354
  1628.7 64.7 %reduce-scatter.18.cloned.1.call-done = f32[64,512]{1,0:T(8,128)} async-done(((f32[1024,512]{1,0:T(8,128)}), f32[64,512]{1,0:T(8,128)}) %reduce-scatter.18.cloned.1.call-update) | async-done | bytes 131088 | tf_op jit(solution)/shard_map/reduce_scatter | solution.py:355
  1693.4 65.2 %reduce-scatter.20.cloned.1.call-done = f32[64,512]{1,0:T(8,128)} async-done(((f32[1024,512]{1,0:T(8,128)}), f32[64,512]{1,0:T(8,128)}) %reduce-scatter.20.cloned.1.call-update) | async-done | bytes 131088 | tf_op jit(solution)/shard_map/reduce_scatter | solution.py:356
  1758.7 144.0 %reduce-scatter.22.cloned.1.call-done = f32[32,1024]{1,0:T(8,128)} async-done(((f32[1024,1024]{1,0:T(8,128)}), f32[32,1024]{1,0:T(8,128)}) %reduce-scatter.22.cloned.1.call-update) | async-done | bytes 131088 | tf_op jit(solution)/shard_map/reduce_scatter | solution.py:370
  1902.7 356.8 %reduce-scatter.24.cloned.1.call-done = f32[32,4096]{1,0:T(8,128)} async-done(((f32[1024,4096]{1,0:T(8,128)}), f32[32,4096]{1,0:T(8,128)}) %reduce-scatter.24.cloned.1.call-update) | async-done | bytes 524304 | tf_op jit(solution)/shard_map/reduce_scatter | solution.py:371
  2259.5 361.4 %reduce-scatter.26.cloned.1.call-done = f32[128,1024]{1,0:T(8,128)} async-done(((f32[4096,1024]{1,0:T(8,128)}), f32[128,1024]{1,0:T(8,128)}) %reduce-scatter.26.cloned.1.call-update) | async-done | bytes 524304 | tf_op jit(solution)/shard_map/reduce_scatter | solution.py:372
  (556 shorter events, 813.0 us)
Async XLA Ops:
  7.2 1297.7 %copy-start = (bf16[1,170,1024]{2,1,0:T(8,128)(2,1)S(1)}, bf16[1,170,1024]{2,1,0:T(8,128)(2,1)}, u32[]{:S(2)}) copy-start(bf16[1,170,1024]{2,1,0:T(8,128)(2,1)} %param.47) | copy-start | bytes 1044484
  7.2 133.9 %all-gather.20.cloned.1.call-start = ((), (), s32[]{:S(2)}) async-start(), calls=%async_computation.15 | async-start | bytes 1114112 | tf_op jit(solution)/shard_map/all_gather | solution.py:93
  7.9 138.3 %all-gather.14.cloned.1.call-start = ((), (), s32[]{:S(2)}) async-start(), calls=%async_computation.12 | async-start | bytes 1114112 | tf_op jit(solution)/shard_map/all_gather | solution.py:90
  8.7 137.6 %all-gather.16.cloned.1.call-start = ((), (), s32[]{:S(2)}) async-start(), calls=%async_computation.13 | async-start | bytes 1114112 | tf_op jit(solution)/shard_map/all_gather | solution.py:91
  9.4 158.5 %all-gather.18.cloned.1.call-start = ((), (), s32[]{:S(2)}) async-start(), calls=%async_computation.14 | async-start | bytes 1114112 | tf_op jit(solution)/shard_map/all_gather | solution.py:92
  10.0 191.4 %all-gather.12.cloned.1.call-start = ((), (), s32[]{:S(2)}) async-start(), calls=%async_computation.11 | async-start | bytes 3145728 | tf_op jit(solution)/shard_map/all_gather | solution.py:107
  10.6 604.0 %all-gather.22.cloned.1.call-start = ((), (), s32[]{:S(2)}) async-start(), calls=%async_computation.16 | async-start | bytes 2162688 | tf_op jit(solution)/shard_map/all_gather | solution.py:98
  11.2 607.5 %all-gather.24.cloned.1.call-start = ((), (), s32[]{:S(2)}) async-start(), calls=%async_computation.17 | async-start | bytes 8650752 | tf_op jit(solution)/shard_map/all_gather | solution.py:99
  11.9 617.4 %all-gather.26.cloned.1.call-start = ((), (), s32[]{:S(2)}) async-start(), calls=%async_computation.18 | async-start | bytes 8650752 | tf_op jit(solution)/shard_map/all_gather | solution.py:100
  146.2 62.1 %copy-start.3 = (bf16[2,512,1024]{2,1,0:T(8,128)(2,1)S(1)}, bf16[2,512,1024]{2,1,0:T(8,128)(2,1)}, u32[]{:S(2)}) copy-start(bf16[2,512,1024]{2,1,0:T(8,128)(2,1)} %param.29) | copy-start | bytes 6291460
  146.2 62.1 %copy-start.78 = (s32[2]{0:T(128)S(1)}, s32[2]{0:T(128)}, u32[]{:S(2)}) copy-start(s32[2]{0:T(128)} %param.31) | copy-start | bytes 28
  168.0 40.4 %copy-start.18 = (bf16[1024,512]{1,0:T(8,128)(2,1)S(1)}, bf16[1024,512]{1,0:T(8,128)(2,1)}, u32[]{:S(2)}) copy-start(bf16[1024,512]{1,0:T(8,128)(2,1)} %all-gather.18.cloned.1.call-done) | copy-start | bytes 3145732
  208.4 391.4 %copy-start.74 = (bf16[1024]{0:T(1024)(128)(2,1)S(1)}, bf16[1024]{0:T(1024)(128)(2,1)}, u32[]{:S(2)}) copy-start(bf16[1024]{0:T(1024)(128)(2,1)} %get-tuple-element.862) | copy-start | bytes 6148
  208.4 391.4 %copy-start.73 = (bf16[1024]{0:T(1024)(128)(2,1)S(1)}, bf16[1024]{0:T(1024)(128)(2,1)}, u32[]{:S(2)}) copy-start(bf16[1024]{0:T(1024)(128)(2,1)} %get-tuple-element.863) | copy-start | bytes 6148
  596.2 33.2 %copy-start.47 = (f32[1024]{0:T(1024)}, f32[1024]{0:T(1024)S(1)}, u32[]{:S(2)}) copy-start(f32[1024]{0:T(1024)S(1)} %get-tuple-element.1427) | copy-start | bytes 12292
  596.2 18.4 all-to-all-start
  599.8 29.6 %copy-start.64 = (f32[1024]{0:T(1024)}, f32[1024]{0:T(1024)S(1)}, u32[]{:S(2)}) copy-start(f32[1024]{0:T(1024)S(1)} %convert_element_type.415) | copy-start | bytes 12292
  599.8 47.8 %copy-start.54 = (f32[1024]{0:T(1024)}, f32[1024]{0:T(1024)S(1)}, u32[]{:S(2)}) copy-start(f32[1024]{0:T(1024)S(1)} %convert_element_type.414) | copy-start | bytes 12292
  666.3 18.5 all-to-all-start.1
  670.8 724.5 %all-gather.28.cloned.1.call-start = ((), (), s32[]{:S(2)}) async-start(), calls=%async_computation.19 | async-start | bytes 6488064 | tf_op jit(solution)/shard_map/all_gather | solution.py:101
  671.5 818.3 %reduce-scatter.12.cloned.1.call-start = ((), (), s32[]{:S(2)}) async-start(), calls=%async_computation.20 | async-start | bytes 3145728 | tf_op jit(solution)/shard_map/reduce_scatter | solution.py:345
  1303.1 195.4 %reduce-scatter.28.cloned.1.call-start = ((), (), s32[]{:S(2)}) async-start(), calls=%async_computation.28 | async-start | bytes 12976128 | tf_op jit(solution)/shard_map/reduce_scatter | solution.py:373
  1311.7 251.7 %reduce-scatter.14.cloned.1.call-start = ((), (), s32[]{:S(2)}) async-start(), calls=%async_computation.21 | async-start | bytes 2228224 | tf_op jit(solution)/shard_map/reduce_scatter | solution.py:353
  1325.0 303.6 %reduce-scatter.16.cloned.1.call-start = ((), (), s32[]{:S(2)}) async-start(), calls=%async_computation.22 | async-start | bytes 2228224 | tf_op jit(solution)/shard_map/reduce_scatter | solution.py:354
  1332.7 360.7 %reduce-scatter.18.cloned.1.call-start = ((), (), s32[]{:S(2)}) async-start(), calls=%async_computation.23 | async-start | bytes 2228224 | tf_op jit(solution)/shard_map/reduce_scatter | solution.py:355
  1341.6 417.1 %reduce-scatter.20.cloned.1.call-start = ((), (), s32[]{:S(2)}) async-start(), calls=%async_computation.24 | async-start | bytes 2228224 | tf_op jit(solution)/shard_map/reduce_scatter | solution.py:356
  1360.5 542.2 %reduce-scatter.22.cloned.1.call-start = ((), (), s32[]{:S(2)}) async-start(), calls=%async_computation.25 | async-start | bytes 4325376 | tf_op jit(solution)/shard_map/reduce_scatter | solution.py:370
  1365.2 894.3 %reduce-scatter.24.cloned.1.call-start = ((), (), s32[]{:S(2)}) async-start(), calls=%async_computation.26 | async-start | bytes 17301504 | tf_op jit(solution)/shard_map/reduce_scatter | solution.py:371
  1376.6 1244.3 %reduce-scatter.26.cloned.1.call-start = ((), (), s32[]{:S(2)}) async-start(), calls=%async_computation.27 | async-start | bytes 17301504 | tf_op jit(solution)/shard_map/reduce_scatter | solution.py:372
  1400.7 89.1 %copy-start.22 = (f32[1,512,1024]{2,1,0:T(8,128)S(1)}, f32[1,512,1024]{2,1,0:T(8,128)}, u32[]{:S(2)}) copy-start(f32[1,512,1024]{2,1,0:T(8,128)} %copy-done.21) | copy-start | bytes 6291460
  1400.7 89.1 %copy-start.38 = (bf16[1,512,1024]{2,1,0:T(8,128)(2,1)S(1)}, bf16[1,512,1024]{2,1,0:T(8,128)(2,1)}, u32[]{:S(2)}) copy-start(bf16[1,512,1024]{2,1,0:T(8,128)(2,1)} %param.46) | copy-start | bytes 3145732
  1400.7 89.1 %copy-start.51 = (f32[512]{0:T(512)S(1)}, f32[512]{0:T(512)}, u32[]{:S(2)}) copy-start(f32[512]{0:T(512)} %copy-done.50) | copy-start | bytes 6148
  (119 other events, 767.5 us)
Sparse Core Ops, SparseCore 0:
  10.2 40.6 all-gather.19
  53.1 36.7 all-gather.13
  92.1 36.9 all-gather.15
  131.1 36.8 all-gather.17
  169.3 32.0 all-gather.11
  204.2 56.5 all-gather.21
  263.8 76.2 all-gather.23
  343.1 75.8 all-gather.25
  674.5 70.8 all-gather.27
  1303.2 31.4 reduce-scatter.11
  1342.3 156.0 reduce-scatter.27
  1502.6 60.6 reduce-scatter.13
  1568.1 60.5 reduce-scatter.15
  1632.8 60.5 reduce-scatter.17
  1698.0 60.5 reduce-scatter.19
  1761.4 141.2 reduce-scatter.21
  1905.4 354.0 reduce-scatter.23
  2262.2 358.6 reduce-scatter.25
where the time goes:
time: 2640 us; the launch traced here: 2630 us
  waiting for transfers between devices  1220 us (46%)
  local copies, waits for them, and re-layouts  716 us (27%)
  matrix products  354 us (13%)
  blocking collectives  155 us (6%)
  other arithmetic  129 us (5%)
    while x192, local copies, waits for them, and re-layouts  404 us
    reduce_scatter x1, waiting for transfers between devices, body(): lax.psum_scatter(down_grad, ('dp', 'head'), scatter_dimension=0, tiled=True)  361 us
    reduce_scatter x1, waiting for transfers between devices, body(): lax.psum_scatter(up_grad, ('dp', 'head'), scatter_dimension=0, tiled=True)  357 us
    reduce_scatter x1, waiting for transfers between devices, body(): lax.psum_scatter(out_grad, ('dp', 'head'), scatter_dimension=0, tiled=True)  144 us
    reshape x6, local copies, waits for them, and re-layouts, skew_rows(): selected.reshape(head_count, seg_len, context + seg_len - 1)[:, :, :context]  120 us
    unnamed x3, blocking collectives  115 us
    reduce_scatter x1, waiting for transfers between devices, body(): lax.psum_scatter(key_grad, 'dp', scatter_dimension=0, tiled=True)  65.3 us
    reduce_scatter x1, waiting for transfers between devices, body(): lax.psum_scatter(place_weight_grad, 'dp', scatter_dimension=0, tiled=True)  65.2 us
  transfers between devices with their start and end apart: 20, of which 12 were waited for; matrix products, arithmetic and copies ran while one was open for 43% of the time, Pallas kernels for 0%

commit v1 on v0

v1 whole, which is shorter than its diff:
```python
import functools
import math

import jax
import jax.numpy as jnp
import numpy as np
from jax import lax
from jax.experimental import pallas as pl
from jax.experimental.pallas import tpu as pltpu
from jax.sharding import PartitionSpec as P

F32 = jnp.float32
BF16 = jnp.bfloat16
MESH = pl.DeviceIdType.MESH
VMEM_LIMIT = 62 * 1024 * 1024
HALF = 256
LANES = 512
SMALL = 16


def dot(a, b):
    return lax.dot_general(a, b, (((1,), (0,)), ((), ())), preferred_element_type=F32)


def dot_nt(a, b):
    return lax.dot_general(a, b, (((1,), (1,)), ((), ())), preferred_element_type=F32)


def dot_tn(a, b):
    return lax.dot_general(a, b, (((0,), (0,)), ((), ())), preferred_element_type=F32)


def position_rows(context, width, used):
    distance = np.arange(context, dtype=np.float32)[:, None]
    frequency = np.exp(
        np.arange(width // 2, dtype=np.float32) * np.float32(-2.0 * math.log(10000.0) / width)
    )
    phases = distance * frequency[None, :].astype(np.float32)
    table = np.concatenate([np.sin(phases), np.cos(phases)], axis=1)
    return table[::-1][context - used :].astype(jnp.bfloat16)


def place(n):
    me = lax.axis_index("dp")
    core = lax.rem(me, 2)
    low = lax.rem(me // 2, 2)
    high = me // 4
    return core, low, high, n // 4


def meet(core, low, high, nhi, more=0):
    barrier = pltpu.get_barrier_semaphore()

    def tell(index):
        pl.semaphore_signal(barrier, inc=1, device_id={"dp": index}, device_id_type=MESH)

    for k in range(1, nhi):
        tell(lax.rem(high + k, nhi) * 4 + low * 2 + core)
    tell(high * 4 + (1 - low) * 2 + core)
    tell(high * 4 + low * 2 + (1 - core))
    pl.semaphore_wait(barrier, nhi + 1 + more)


def remote(src, dst, send, recv, index):
    return pltpu.make_async_remote_copy(
        src_ref=src,
        dst_ref=dst,
        send_sem=send,
        recv_sem=recv,
        device_id={"dp": index},
        device_id_type=MESH,
    )


class Gather:
    def __init__(self, n, pairs, sems):
        self.core, self.low, self.high, self.nhi = place(n)
        self.pairs = pairs
        (self.zs, self.zr, self.ys, self.yr, self.cs, self.cr, self.own) = sems

    def z_copies(self, c):
        shard, whole = self.pairs[c]
        return [
            remote(
                shard,
                whole.at[self.high, self.low, self.core],
                self.zs.at[c, k - 1],
                self.zr.at[c, k - 1],
                lax.rem(self.high + k, self.nhi) * 4 + self.low * 2 + self.core,
            )
            for k in range(1, self.nhi)
        ]

    def own_copy(self, c):
        shard, whole = self.pairs[c]
        return pltpu.make_async_copy(
            shard, whole.at[self.high, self.low, self.core], self.own.at[c]
        )

    def y_copy(self, c):
        _, whole = self.pairs[c]
        part = whole.at[:, self.low, self.core]
        return remote(
            part,
            part,
            self.ys.at[c],
            self.yr.at[c],
            self.high * 4 + (1 - self.low) * 2 + self.core,
        )

    def c_copy(self, c):
        _, whole = self.pairs[c]
        part = whole.at[:, :, self.core]
        return remote(
            part,
            part,
            self.cs.at[c],
            self.cr.at[c],
            self.high * 4 + self.low * 2 + (1 - self.core),
        )

    def start(self, c):
        for copy in self.z_copies(c):
            copy.start()
        self.own_copy(c).start()

    def pass_y(self, c):
        self.own_copy(c).wait()
        for copy in self.z_copies(c):
            copy.wait_recv()
        self.y_copy(c).start()

    def pass_core(self, c):
        self.y_copy(c).wait_recv()
        self.c_copy(c).start()

    def arrive(self, c):
        self.c_copy(c).wait_recv()

    def close(self, c):
        for copy in self.z_copies(c):
            copy.wait_send()
        self.y_copy(c).wait_send()
        self.c_copy(c).wait_send()

    @staticmethod
    def semaphores(count, nhi):
        dma = pltpu.SemaphoreType.DMA
        return [
            dma((count, nhi - 1)),
            dma((count, nhi - 1)),
            dma((count,)),
            dma((count,)),
            dma((count,)),
            dma((count,)),
            dma((count,)),
        ]


class Scatter:
    def __init__(self, n, items, mine, mine_sem, sems):
        self.core, self.low, self.high, self.nhi = place(n)
        self.items = items
        self.mine, self.mine_sem = mine, mine_sem
        (self.cs, self.cr, self.ys, self.yr, self.zs, self.zr) = sems

    def c_copy(self, c):
        return remote(
            self.items[c][0].at[:, :, 1 - self.core],
            self.items[c][2],
            self.cs.at[c],
            self.cr.at[c],
            self.high * 4 + self.low * 2 + (1 - self.core),
        )

    def mine_copy(self, c):
        slot = c % 2
        return pltpu.make_async_copy(
            self.items[c][0].at[:, :, self.core], self.mine.at[slot], self.mine_sem.at[slot]
        )

    def y_copy(self, c):
        return remote(
            self.items[c][2].at[:, 1 - self.low],
            self.items[c][3],
            self.ys.at[c],
            self.yr.at[c],
            self.high * 4 + (1 - self.low) * 2 + self.core,
        )

    def z_copies(self, c):
        return [
            remote(
                self.items[c][3].at[lax.rem(self.high + k, self.nhi)],
                self.items[c][4].at[k - 1],
                self.zs.at[c, k - 1],
                self.zr.at[c, k - 1],
                lax.rem(self.high + k, self.nhi) * 4 + self.low * 2 + self.core,
            )
            for k in range(1, self.nhi)
        ]

    def start(self, c):
        self.c_copy(c).start()
        if not self.items[c][1]:
            self.mine_copy(c).start()

    def add_core(self, c):
        here = self.items[c][1]
        if not here:
            self.mine_copy(c).wait()
        self.c_copy(c).wait_recv()
        land = self.items[c][2]

        def body(i, carry):
            for j in range(2):
                own = self.items[c][0][i, j, self.core] if here else self.mine[c % 2, i, j]
                land[i, j] = (land[i, j].astype(F32) + own.astype(F32)).astype(BF16)
            return carry

        lax.fori_loop(0, self.nhi, body, 0)
        self.y_copy(c).start()

    def add_y(self, c):
        self.y_copy(c).wait_recv()
        src, land = self.items[c][2], self.items[c][3]

        def body(i, carry):
            land[i] = (land[i].astype(F32) + src[i, self.low].astype(F32)).astype(BF16)
            return carry

        lax.fori_loop(0, self.nhi, body, 0)
        for copy in self.z_copies(c):
            copy.start()

    def add_z(self, c):
        for copy in self.z_copies(c):
            copy.wait_recv()
        land, last, done = self.items[c][3:]
        total = land[self.high].astype(F32)
        for k in range(self.nhi - 1):
            total = total + last[k].astype(F32)
        done(total)

    def tick(self, t):
        count = len(self.items)
        if 0 <= t - 1 < count:
            self.add_core(t - 1)
        if t < count:
            self.start(t)
        if 0 <= t - 2 < count:
            self.add_y(t - 2)
        if 0 <= t - 3 < count:
            self.add_z(t - 3)

    def close(self, c):
        self.c_copy(c).wait_send()
        self.y_copy(c).wait_send()
        for copy in self.z_copies(c):
            copy.wait_send()

    @staticmethod
    def scratch(count, nhi, rows):
        dma = pltpu.SemaphoreType.DMA
        return [
            pltpu.VMEM((count, nhi, 2, rows, LANES), BF16),
            pltpu.VMEM((count, nhi, rows, LANES), BF16),
            pltpu.VMEM((count, nhi - 1, rows, LANES), BF16),
            pltpu.VMEM((2, nhi, 2, rows, LANES), BF16),
            dma((2,)),
            dma((count,)),
            dma((count,)),
            dma((count,)),
            dma((count,)),
            dma((count, nhi - 1)),
            dma((count, nhi - 1)),
        ]


def norm_rows(values):
    mean = jnp.mean(values, axis=-1, keepdims=True)
    centred = values - mean
    variance = jnp.mean(centred * centred, axis=-1, keepdims=True)
    return centred * lax.rsqrt(variance + 1e-05)


def attend_rows(query_content, query_place, keys, place_keys, first_seen, last_seen, scale):
    width = keys.shape[0]
    content = dot_nt(query_content, keys)
    by_place = pltpu.roll(
        dot_nt(query_place, place_keys), width - (HALF - 1), 1, stride=1, stride_axis=0
    )
    column = lax.broadcasted_iota(jnp.int32, (HALF, width), 1)
    seen = (column >= first_seen) & (column <= last_seen)
    scores = jnp.where(seen, (content + by_place) * (scale * math.log2(math.e)), -1e30)
    top = jnp.max(scores, axis=1, keepdims=True)
    expo = jnp.exp2(scores - top)
    return expo * (1.0 / jnp.sum(expo, axis=1, keepdims=True))


def forward_kernel(
    n,
    past,
    seg_len,
    docs,
    compressed,
    memory,
    segment,
    cotangent,
    query_w,
    key_w,
    value_w,
    place_w,
    out_w,
    up_parts,
    down_w,
    comp_w,
    small,
    table,
    attended,
    seg_other,
    cot_other,
    params,
    kv_out,
    q_out,
    wide_out,
    near_out,
    place_out,
    xhat_out,
    query_whole,
    key_whole,
    value_whole,
    place_whole,
    out_whole,
    up_whole,
    down_whole,
    comp_whole,
    small_whole,
    out_shard,
    up_shard,
    comp_shard,
    small_shard,
    normed,
    past_rows,
    seg_rows,
    flat,
    small_rows,
    att,
    load_sem,
    flat_sem,
    own_sem,
    pair_send,
    pair_recv,
    att_own,
    att_send,
    att_recv,
    *sems,
):
    step = pl.program_id(0)
    x = lax.axis_index("head")
    core, low, high, nhi = place(n)
    tile = 256
    width = normed.shape[2]
    context = past + seg_len
    head = jnp.maximum(step - 2, 0) // 2
    half = comp_w.shape[1] // 2

    items = [(small_shard, small_whole)]
    items += [(query_w, query_whole), (key_w, key_whole), (value_w, value_whole), (place_w, place_whole)]
    items += [(out_shard, out_whole)]
    items += [(up_shard.at[f], up_whole.at[f]) for f in range(4)]
    mid = down_w.shape[0] // 2
    for part in range(2):
        at = pl.ds(part * mid, mid)
        items.append((down_w.at[at], down_whole.at[:, :, :, at]))
    items.append((comp_shard, comp_whole))
    gather = Gather(n, items, sems)
    count = len(items)
    needs = {0: 0, 5: 1, 6: 2, 7: 2, 8: 2, 9: 2, 12: 3}

    def pair(src, dst, k):
        return pltpu.make_async_remote_copy(
            src_ref=src,
            dst_ref=dst,
            send_sem=pair_send.at[k],
            recv_sem=pair_recv.at[k],
            device_id={"head": 1 - x},
            device_id_type=MESH,
        )

    mine_at = pl.ds(pl.multiple_of(x * half, half), half)
    other_at = pl.ds(pl.multiple_of((1 - x) * half, half), half)
    pairs = [
        pair(small, small_shard.at[x], 0),
        pair(out_w, out_shard.at[x], 1),
        pair(up_parts.at[1 - x], up_shard.at[:, x], 2),
        pair(comp_w.at[:, other_at], comp_shard.at[x], 3),
        pair(segment.at[0], seg_other, 4),
        pair(cotangent.at[0], cot_other, 5),
    ]
    owns = [
        pltpu.make_async_copy(small, small_shard.at[x], own_sem.at[0]),
        pltpu.make_async_copy(out_w, out_shard.at[x], own_sem.at[1]),
        pltpu.make_async_copy(up_parts.at[x], up_shard.at[:, x], own_sem.at[2]),
        pltpu.make_async_copy(comp_w.at[:, mine_at], comp_shard.at[x], own_sem.at[3]),
    ]
    loads = []
    for i in range(2):
        s = lax.rem(x + i, 2)
        loads.append(pltpu.make_async_copy(compressed.at[s], past_rows.at[i, 0], load_sem.at[i, 0]))
        loads.append(pltpu.make_async_copy(memory.at[s], past_rows.at[i, 1], load_sem.at[i, 1]))
    loads.append(pltpu.make_async_copy(segment.at[0], seg_rows.at[0], load_sem.at[0, 2]))
    load_other = pltpu.make_async_copy(seg_other, seg_rows.at[1], load_sem.at[1, 2])

    joined = set()

    def join(k):
        if k not in joined:
            joined.add(k)
            owns[k].wait()
            pairs[k].wait_recv()

    def tick(t):
        lead = t + 4
        if lead < count:
            if lead in needs:
                join(needs[lead])
            gather.start(lead)
        if t < count:
            gather.pass_y(t)
        if 0 <= t - 1 < count:
            gather.pass_core(t - 1)
        if 0 <= t - 2 < count:
            gather.arrive(t - 2)

    def flat_copies(h, slot):
        at = pl.ds(h * 128, 128)
        return [
            pltpu.make_async_copy(
                whole.at[:, :, :, :, at],
                flat.at[slot, :, :, :, :, pl.ds(j * 128, 128)],
                flat_sem.at[slot, j],
            )
            for j, whole in enumerate((query_whole, key_whole, value_whole, place_whole))
        ]

    def norm_into(i, values, at):
        eye = (
            lax.broadcasted_iota(jnp.int32, (tile, tile), 0)
            == lax.broadcasted_iota(jnp.int32, (tile, tile), 1)
        ).astype(BF16)
        gain = jnp.concatenate([params[0:1, :], params[1:2, :]], axis=1)
        shift = jnp.concatenate([params[2:3, :], params[3:4, :]], axis=1)
        xhat = norm_rows(values.astype(F32))
        normed[i, pl.ds(at, tile)] = (xhat * gain + shift).astype(BF16)
        xhat = xhat.astype(BF16)
        for b in range(width // tile):
            xhat_out[i, b * tile : (b + 1) * tile, pl.ds(at, tile)] = dot_nt(
                eye, xhat[:, b * tile : (b + 1) * tile]
            ).astype(BF16)

    def norm_past(i):
        per = past // 2 // tile

        def one(k, carry):
            at = pl.multiple_of(k * tile, tile)
            inner = pl.multiple_of(lax.rem(k, per) * tile, tile)
            norm_into(i, past_rows[i, k // per, pl.ds(inner, tile)], at)
            return carry

        lax.fori_loop(0, past // tile, one, 0)

    def norm_segment(i):
        def one(k, carry):
            at = pl.multiple_of(k * tile, tile)
            norm_into(i, seg_rows[i, pl.ds(at, tile)], past + at)
            return carry

        lax.fori_loop(0, seg_len // tile, one, 0)

    @pl.when(step == 0)
    def _():
        barrier = pltpu.get_barrier_semaphore()
        pl.semaphore_signal(
            barrier, inc=1, device_id={"head": 1 - x}, device_id_type=MESH
        )
        meet(core, low, high, nhi, 1)
        for k in (0, 1, 2):
            pairs[k].start()
            owns[k].start()
        for copy in loads:
            copy.start()
        for c in range(1, 4):
            gather.start(c)
        join(0)
        gather.start(0)
        for k in (4, 3, 5):
            pairs[k].start()
        owns[3].start()
        tick(0)
        tick(1)
        tick(2)
        summed = pltpu.make_async_copy(small_whole, small_rows, load_sem.at[0, 3])
        summed.start()
        summed.wait()
        both = jnp.sum(small_rows[...].reshape(n, 2, SMALL, LANES).astype(F32), axis=0)
        row = lax.broadcasted_iota(jnp.int32, (SMALL, LANES), 0)
        by_head = jnp.where(x == 0, both[0], both[1])
        params[...] = jnp.where(row < 8, both[0] + both[1], by_head)
        for copy in (loads[0], loads[1], loads[4]):
            copy.wait()
        norm_past(0)
        tick(3)
        norm_segment(0)
        tick(4)

    @pl.when(step == 1)
    def _():
        for copy in loads[2:4]:
            copy.wait()
        norm_past(1)
        tick(5)
        tick(6)
        for copy in flat_copies(0, 0):
            copy.start()

    for k in range(2, 10):

        @pl.when(step == k)
        def _(k=k):
            tick(k + 5)
            h, slot = (k - 2) // 2, ((k - 2) // 2) % 2
            if k % 2 == 0:
                for copy in flat_copies(h, slot):
                    copy.wait()
                if h < 3:
                    for copy in flat_copies(h + 1, 1 - slot):
                        copy.start()
            if k == 3:
                pairs[4].wait_recv()
                load_other.start()
                load_other.wait()
                norm_segment(1)

    def att_pair(h, i):
        at = pl.ds(pl.multiple_of(x * LANES + h * 128, 128), 128)
        return pltpu.make_async_remote_copy(
            src_ref=att.at[h, i],
            dst_ref=attended.at[1 - i, :, at],
            send_sem=att_send.at[h, i],
            recv_sem=att_recv.at[h, i],
            device_id={"head": 1 - x},
            device_id_type=MESH,
        )

    def att_local(h, i):
        at = pl.ds(pl.multiple_of(x * LANES + h * 128, 128), 128)
        return pltpu.make_async_copy(att.at[h, i], attended.at[i, :, at], att_own.at[h, i])

    @pl.when(step >= 2)
    def _():
        i = lax.rem(step, 2)
        s = lax.rem(x + i, 2)
        slot = lax.rem(head, 2)

        def weights(a, b):
            return flat[slot, :, :, :, :, a:b].reshape(width, b - a)

        @pl.when(i == 0)
        def _():
            mat = weights(384, 512)
            for k in range(table.shape[0] // tile):
                place_out[0, k * tile : (k + 1) * tile] = dot(
                    table[k * tile : (k + 1) * tile], mat
                ).astype(BF16)

        mat = weights(128, 384)
        for k in range(context // tile):
            kv_out[0, 0, k * tile : (k + 1) * tile] = dot(
                normed[i, pl.ds(k * tile, tile)], mat
            ).astype(BF16)
        mat = weights(0, 128)
        bias_at = pl.ds(pl.multiple_of(head * 128, 128), 128)
        for k in range(seg_len // tile):
            queries = dot(normed[i, pl.ds(past + k * tile, tile)], mat)
            at = slice(k * tile, (k + 1) * tile)
            q_out[0, 0, at, 0:128] = (queries + params[8:9, bias_at]).astype(BF16)
            q_out[0, 0, at, 128:256] = (queries + params[9:10, bias_at]).astype(BF16)

        scale = 1.0 / math.sqrt(128)
        for part, out, key_start, key_count, place_start in (
            (0, wide_out, 0, past + HALF, 0),
            (1, near_out, past, seg_len, past - HALF),
        ):
            token = lax.broadcasted_iota(jnp.int32, (HALF, 1), 0) + part * HALF
            first = jnp.where(token >= docs[s, 0], past + docs[s, 0], past - docs[s, 3])
            first = jnp.where(token >= docs[s, 1], past + docs[s, 1], first)
            first = jnp.where(token >= docs[s, 2], past + docs[s, 2], first)
            at = slice(part * HALF, (part + 1) * HALF)
            weights_low = attend_rows(
                q_out[0, 0, at, 0:128],
                q_out[0, 0, at, 128:256],
                kv_out[0, 0, key_start : key_start + key_count, 0:128],
                place_out[0, place_start : place_start + key_count],
                first - key_start,
                token + (past - key_start),
                scale,
            ).astype(BF16)
            out[0, 0] = weights_low
            att[head, i, at] = dot(
                weights_low, kv_out[0, 0, key_start : key_start + key_count, 128:256]
            ).astype(BF16)
        att_pair(head, i).start()
        att_local(head, i).start()

    @pl.when(step == pl.num_programs(0) - 1)
    def _():
        for t in range(15, count + 2):
            tick(t)
        for h in range(4):
            for i in range(2):
                att_local(h, i).wait()
                att_pair(h, i).wait()
        for copy in pairs:
            copy.wait_send()
        pairs[5].wait_recv()
        for c in range(count):
            gather.close(c)


def attention_forward(
    n, docs, compressed, memory, segment, cotangent, mats, out_w, up_parts, down_w, comp_w, small, table
):
    _, seg_len, width = segment.shape
    past = compressed.shape[1] + memory.shape[1]
    context = past + seg_len
    nhi = n // 4
    lead = (nhi, 2, 2)
    half_rows = out_w.shape[0]
    comp_rows = comp_w.shape[0]
    any_spec = pl.BlockSpec(memory_space=pl.ANY)
    single = pl.Buffered(1)
    bf = lambda *shape: jax.ShapeDtypeStruct(shape, BF16)
    head = lambda t: jnp.maximum(t - 2, 0) // 2
    which = lambda t: lax.rem(jnp.maximum(t, 2), 2)
    by_both = lambda t: (head(t), which(t), 0, 0)
    dma = pltpu.SemaphoreType.DMA
    count = 13
    return pl.pallas_call(
        functools.partial(forward_kernel, n, past, seg_len),
        grid=(10,),
        out_shape=(
            bf(2, seg_len, width),
            bf(seg_len, width),
            bf(seg_len, width),
            jax.ShapeDtypeStruct((SMALL, LANES), F32),
            bf(4, 2, context, 256),
            bf(4, 2, seg_len, 256),
            bf(4, 2, HALF, past + HALF),
            bf(4, 2, HALF, seg_len),
            bf(4, past + HALF, 128),
            bf(2, width, context),
            *[bf(*lead, *w.shape) for w in mats],
            bf(*lead, 2, half_rows, width),
            bf(4, *lead, 2, half_rows, LANES),
            bf(*lead, *down_w.shape),
            bf(*lead, 2, comp_rows, LANES),
            bf(*lead, 2, SMALL, LANES),
            bf(2, half_rows, width),
            bf(4, 2, half_rows, LANES),
            bf(2, comp_rows, LANES),
            bf(2, SMALL, LANES),
        ),
        in_specs=[pl.BlockSpec(memory_space=pltpu.SMEM)]
        + [any_spec] * 13
        + [pl.BlockSpec(table.shape, lambda t: (0, 0), pipeline_mode=single)],
        out_specs=(
            any_spec,
            any_spec,
            any_spec,
            pl.BlockSpec((SMALL, LANES), lambda t: (0, 0)),
            pl.BlockSpec((1, 1, context, 256), by_both),
            pl.BlockSpec((1, 1, seg_len, 256), by_both),
            pl.BlockSpec((1, 1, HALF, past + HALF), by_both),
            pl.BlockSpec((1, 1, HALF, seg_len), by_both),
            pl.BlockSpec((1, past + HALF, 128), lambda t: (head(t), 0, 0)),
            pl.BlockSpec((2, width, context), lambda t: (0, 0, 0), pipeline_mode=single),
            *[any_spec] * 13,
        ),
        scratch_shapes=[
            pltpu.VMEM((2, context, width), BF16),
            pltpu.VMEM((2, 2, past // 2, width), BF16),
            pltpu.VMEM((2, seg_len, width), BF16),
            pltpu.VMEM((2,) + lead + (mats[0].shape[0], LANES), BF16),
            pltpu.VMEM(lead + (2, SMALL, LANES), BF16),
            pltpu.VMEM((4, 2, seg_len, 128), BF16),
            dma((2, 4)),
            dma((2, 4)),
            dma((4,)),
            dma((6,)),
            dma((6,)),
            dma((4, 2)),
            dma((4, 2)),
            dma((4, 2)),
        ]
        + Gather.semaphores(count, nhi),
        compiler_params=pltpu.CompilerParams(
            vmem_limit_bytes=VMEM_LIMIT,
            dimension_semantics=("arbitrary",),
            collective_id=0,
            has_side_effects=True,
        ),
        name="attention_forward",
    )(docs, compressed, memory, segment, cotangent, *mats, out_w, up_parts, down_w, comp_w, small, table)


def gelu_parts(v):
    c = math.sqrt(2.0 / math.pi)
    square = v * v
    t = jnp.tanh(c * (v + 0.044715 * square * v))
    half = 0.5 * (1.0 + t)
    slope = half + 0.5 * v * (1.0 - t * t) * (c * (1.0 + 3 * 0.044715 * square))
    return v * half, slope


def feed_kernel(
    att,
    segment,
    cot,
    out_w,
    up,
    down,
    gain,
    shift,
    residual_out,
    branch_out,
    terms_out,
    up_out,
    down_out,
    residual,
    low,
    low_t,
    act,
    pre,
    branch,
    terms,
):
    f = pl.program_id(0)
    tile = 256
    total, width = residual.shape

    @pl.when(f == 0)
    def _():
        eye = (
            lax.broadcasted_iota(jnp.int32, (tile, tile), 0)
            == lax.broadcasted_iota(jnp.int32, (tile, tile), 1)
        ).astype(BF16)

        def project(i, carry):
            at = pl.ds(pl.multiple_of(i * tile, tile), tile)
            residual[at, :] = segment[at, :].astype(F32) + dot(att[at, :], out_w[...])
            return carry

        lax.fori_loop(0, total // tile, project, 0)
        for i in range(total // tile):
            at = slice(i * tile, (i + 1) * tile)
            value = (norm_rows(residual[at, :]) * gain[...] + shift[...]).astype(BF16)
            low[at, :] = value
            for b in range(width // tile):
                low_t[b * tile : (b + 1) * tile, at] = dot_nt(
                    eye, value[:, b * tile : (b + 1) * tile]
                ).astype(BF16)
        residual_out[...] = residual[0 : total // 2, :]
        branch[...] = jnp.zeros_like(branch)
        terms[...] = jnp.zeros_like(terms)

    def rows_body(i, carry):
        at = pl.ds(pl.multiple_of(i * tile, tile), tile)
        value, slope = gelu_parts(dot(low[at, :], up[0]))
        value = value.astype(BF16)
        act[at, :] = value
        back = dot_nt(cot[at, :], down[...]).astype(BF16).astype(F32)
        back = (back * slope).astype(BF16)
        pre[at, :] = back
        branch[at, :] += dot(value, down[...])
        terms[at, :] += dot_nt(back, up[0])
        return carry

    lax.fori_loop(0, total // tile, rows_body, 0)

    for i in range(width // tile):
        at = slice(i * tile, (i + 1) * tile)
        up_out[0, at, :] = dot(low_t[at, :], pre[...]).astype(BF16)
    for i in range(LANES // tile):
        at = slice(i * tile, (i + 1) * tile)
        down_out[at, :] = dot_tn(act[:, at], cot[...]).astype(BF16)

    @pl.when(f == pl.num_programs(0) - 1)
    def _():
        branch_out[...] = branch[...].astype(BF16)
        terms_out[...] = terms[...].astype(BF16)


def feed_forward(att, segment, cot, out_w, up, down, gain, shift):
    total, width = segment.shape
    const2 = lambda f: (0, 0)
    single = pl.Buffered(1)
    full = lambda: pl.BlockSpec((total, width), const2, pipeline_mode=single)
    return pl.pallas_call(
        feed_kernel,
        grid=(4,),
        out_shape=(
            jax.ShapeDtypeStruct((total // 2, width), F32),
            jax.ShapeDtypeStruct((total, width), BF16),
            jax.ShapeDtypeStruct((total, width), BF16),
            jax.ShapeDtypeStruct((4, width, LANES), BF16),
            jax.ShapeDtypeStruct((4 * LANES, width), BF16),
        ),
        in_specs=[
            full(),
            full(),
            full(),
            pl.BlockSpec((width, width), const2, pipeline_mode=single),
            pl.BlockSpec((1, width, LANES), lambda f: (f, 0, 0)),
            pl.BlockSpec((LANES, width), lambda f: (f, 0)),
            pl.BlockSpec((1, width), const2),
            pl.BlockSpec((1, width), const2),
        ],
        out_specs=(
            pl.BlockSpec((total // 2, width), const2, pipeline_mode=single),
            full(),
            full(),
            pl.BlockSpec((1, width, LANES), lambda f: (f, 0, 0)),
            pl.BlockSpec((LANES, width), lambda f: (f, 0)),
        ),
        scratch_shapes=[
            pltpu.VMEM((total, width), F32),
            pltpu.VMEM((total, width), BF16),
            pltpu.VMEM((width, total), BF16),
            pltpu.VMEM((total, LANES), BF16),
            pltpu.VMEM((total, LANES), BF16),
            pltpu.VMEM((total, width), F32),
            pltpu.VMEM((total, width), F32),
        ],
        compiler_params=pltpu.CompilerParams(
            vmem_limit_bytes=VMEM_LIMIT, dimension_semantics=("arbitrary",)
        ),
        name="feed_forward",
    )(att, segment, cot, out_w, up, down, gain, shift)


def norm_back(xhat, rstd, grad):
    a = jnp.mean(grad, axis=-1, keepdims=True)
    b = jnp.mean(grad * xhat, axis=-1, keepdims=True)
    return rstd * (grad - a - xhat * b)


def backward_kernel(
    n,
    past,
    seg_len,
    dout,
    kv,
    q,
    wide,
    near,
    place_keys,
    xhat_t,
    query_w,
    key_w,
    value_w,
    table_t,
    gain_row,
    gain_col,
    shift_col,
    segment,
    residual_grad,
    small_in,
    comp,
    up,
    down,
    out,
    segment_out,
    query_out,
    key_out,
    value_out,
    place_out,
    out_out,
    up_out,
    down_out,
    comp_out,
    small_out,
    flat,
    raw,
    sums,
    place_sum,
    input_grad,
    dkv,
    gain_sum,
    shift_sum,
    head_grads,
    context_land,
    context_send,
    up_send,
    up_land,
    comp_stage,
    comp_send,
    comp_land,
    out_keep,
    out_send,
    out_land,
    small_mine,
    small_c,
    small_y,
    small_z,
    small_x,
    pair_send,
    pair_recv,
    small_send,
    small_recv,
    land_c,
    land_y,
    land_z,
    mine,
    mine_sem,
    *sems,
):
    step = pl.program_id(0)
    x = lax.axis_index("head")
    core, low, high, nhi = place(n)
    head = lax.rem(step, 4)
    tile = 256
    context = past + seg_len
    width = flat.shape[0]
    rows = width // n
    half_rows = rows // 2
    comp_rows = comp_send.shape[0]
    scale = 1.0 / math.sqrt(128)
    flip = (
        lax.broadcasted_iota(jnp.int32, (HALF, HALF), 0)
        + lax.broadcasted_iota(jnp.int32, (HALF, HALF), 1)
        == HALF - 1
    ).astype(BF16)

    def pair(src, dst, k):
        return pltpu.make_async_remote_copy(
            src_ref=src,
            dst_ref=dst,
            send_sem=pair_send.at[k],
            recv_sem=pair_recv.at[k],
            device_id={"head": 1 - x},
            device_id_type=MESH,
        )

    context_pair = pair(context_send, context_land, 0)
    comp_pair = pair(comp_send, comp_land, 1)
    up_pairs = [pair(up_send.at[f], up_land.at[f], 2 + f) for f in range(4)]
    out_pairs = [pair(out_send.at[b], out_land.at[b], 6 + b) for b in range(2)]

    def comp_done(m):
        def done(total):
            comp_stage[m * rows : (m + 1) * rows, :] = total
            if m == 2:
                upper, lower = comp_stage[0:comp_rows, :], comp_stage[comp_rows:, :]
                to = pl.ds(pl.multiple_of(x * LANES, LANES), LANES)
                comp_out[:, to] = jnp.where(x == 0, upper, lower)
                comp_send[...] = jnp.where(x == 0, lower, upper).astype(BF16)
                comp_pair.start()

        return done

    def up_done(f):
        def done(total):
            upper, lower = total[0:half_rows], total[half_rows:]
            up_out[x, f] = jnp.where(x == 0, upper, lower)
            up_send[f] = jnp.where(x == 0, lower, upper).astype(BF16)
            up_pairs[f].start()

        return done

    def down_done(a, b):
        def done(total):
            down_out[a * rows : (a + 1) * rows, b * LANES : (b + 1) * LANES] = total

        return done

    def out_done(b):
        def done(total):
            upper, lower = total[0:half_rows], total[half_rows:]
            out_keep[b] = jnp.where(x == 0, upper, lower)
            out_send[b] = jnp.where(x == 0, lower, upper).astype(BF16)
            out_pairs[b].start()

        return done

    def head_done(h):
        def done(total):
            for j, ref in enumerate((query_out, key_out, value_out, place_out)):
                ref[:, h * 128 : (h + 1) * 128] = total[:, j * 128 : (j + 1) * 128]

        return done

    parts = [
        (comp.at[:, :, :, pl.ds(m * rows, rows)], False, comp_done(m)) for m in range(3)
    ]
    parts += [(up.at[f], False, up_done(f)) for f in range(4)]
    for a in range(2):
        for b in range(2):
            at, to = pl.ds(a * rows, rows), pl.ds(b * LANES, LANES)
            parts.append((down.at[:, :, :, at, to], False, down_done(a, b)))
    parts += [
        (out.at[:, :, :, :, pl.ds(b * LANES, LANES)], False, out_done(b)) for b in range(2)
    ]
    parts += [(head_grads.at[h], True, head_done(h)) for h in range(4)]
    scatter = Scatter(
        n,
        [
            (part, here, land_c.at[c], land_y.at[c], land_z.at[c], done)
            for c, (part, here, done) in enumerate(parts)
        ],
        mine,
        mine_sem,
        sems,
    )
    count = len(parts)

    @pl.when(step == 0)
    def _():
        barrier = pltpu.get_barrier_semaphore()
        pl.semaphore_signal(barrier, inc=1, device_id={"head": 1 - x}, device_id_type=MESH)
        meet(core, low, high, nhi, 1)
        raw[...] = jnp.zeros_like(raw)
        sums[...] = jnp.zeros_like(sums)
        place_sum[...] = jnp.zeros_like(place_sum)
        gain_sum[...] = jnp.zeros_like(gain_sum)
        shift_sum[...] = jnp.zeros_like(shift_sum)
        small_mine[...] = small_in[...]

    @pl.when(head == 0)
    def _():
        input_grad[...] = jnp.zeros_like(input_grad)

    for k in range(8):
        pl.when(step == k)(functools.partial(scatter.tick, 2 * k))

    for j, mat in enumerate((query_w, key_w, value_w)):
        flat[:, j * 128 : (j + 1) * 128] = mat[...]

    query_grads = []
    key_rows = []
    value_rows = []
    place_rows = []
    bias_at = pl.ds(pl.multiple_of(head * 128, 128), 128)
    for part, weights_ref, key_start, key_count, place_start in (
        (0, wide, 0, past + HALF, 0),
        (1, near, past, seg_len, past - HALF),
    ):
        at = slice(part * HALF, (part + 1) * HALF)
        keys_at = slice(key_start, key_start + key_count)
        attn = weights_ref[0, 0]
        grad = dout[0, at]
        value_rows.append(dot_tn(grad, attn))
        weights_grad = dot_nt(grad, kv[0, 0, keys_at, 128:256])
        attn = attn.astype(F32)
        row = jnp.sum(weights_grad * attn, axis=1, keepdims=True)
        scores_grad = (attn * (weights_grad - row) * scale).astype(BF16)
        content_grad = dot(scores_grad, kv[0, 0, keys_at, 0:128]).astype(BF16)
        key_rows.append(dot_tn(q[0, 0, at, 0:128], scores_grad))
        by_place = pltpu.roll(dot(flip, scores_grad), 0, 1, stride=1, stride_axis=0).astype(BF16)
        place_grad = dot(by_place, place_keys[0, place_start : place_start + key_count])
        place_grad = dot(flip, place_grad.astype(BF16)).astype(BF16)
        flipped_q = dot(flip, q[0, 0, at, 128:256]).astype(BF16)
        place_rows.append(dot_tn(flipped_q, by_place))
        content_f = content_grad.astype(F32)
        place_f = place_grad.astype(F32)
        small_mine[8:9, bias_at] += jnp.sum(content_f, axis=0, keepdims=True)
        small_mine[9:10, bias_at] += jnp.sum(place_f, axis=0, keepdims=True)
        query_grads.append((content_f + place_f).astype(BF16))

    for j, (wide_rows, near_rows) in enumerate((key_rows, value_rows)):
        at = slice(j * 128, (j + 1) * 128)
        dkv[at, 0:past] = wide_rows[:, 0:past].astype(BF16)
        dkv[at, past : past + HALF] = (wide_rows[:, past:] + near_rows[:, 0:HALF]).astype(BF16)
        dkv[at, past + HALF :] = near_rows[:, HALF:].astype(BF16)
    split = past - HALF
    for at, rows_grad in (
        (slice(0, split), place_rows[0][:, 0:split]),
        (slice(split, None), place_rows[0][:, split:] + place_rows[1]),
    ):
        place_sum[head, :, at] = (
            place_sum[head, :, at].astype(F32) + rows_grad.astype(BF16).astype(F32)
        ).astype(BF16)
    dq = jnp.concatenate(query_grads, axis=0)
    stacked = jnp.concatenate([dq, dkv[:, past:].astype(F32).T.astype(BF16)], axis=1)

    for k in range(8):
        pl.when(step == k)(functools.partial(scatter.tick, 2 * k + 1))

    ones = jnp.ones((8, context), BF16)
    sums[head, :, 0:128] += dot(ones[:, 0:seg_len], dq)
    sums[head, :, 128:384] += dot_nt(ones, dkv[...])
    for k in range(width // tile):
        at = slice(k * tile, (k + 1) * tile)
        raw[head, at, 0:128] += dot(xhat_t[0, at, past:], dq)
        raw[head, at, 128:384] += dot_nt(xhat_t[0, at, :], dkv[...])
        input_grad[:, at] += dot_nt(stacked, flat[at, 0:384])

    @pl.when(step >= 4)
    def _():
        place_low = place_sum[head]
        block = tile // (4 * rows)
        total = sums[head, 0:1, :]
        for k in range(width // tile):
            at = slice(k * tile, (k + 1) * tile)
            to = slice(k * block, (k + 1) * block)
            got = raw[head, at, :]
            mats = flat[at, 0:384].astype(F32)
            for acc, term in ((gain_sum, mats * got), (shift_sum, mats * total)):
                acc[at, :] += term[:, 0:128] + term[:, 128:256] + term[:, 256:384]
            grad = (gain_col[at, :] * got + shift_col[at, :] * total).astype(BF16)
            head_grads[head, to, :, :, :, 0:384] = grad.reshape(block, 2, 2, rows, 384)
            grad = dot_nt(table_t[at, :], place_low).astype(BF16)
            head_grads[head, to, :, :, :, 384:512] = grad.reshape(block, 2, 2, rows, 128)

    def own_rows(k):
        at = slice(k * tile, (k + 1) * tile)
        values = segment[0, at].astype(F32)
        mean = jnp.mean(values, axis=-1, keepdims=True)
        centred = values - mean
        rstd = lax.rsqrt(jnp.mean(centred * centred, axis=-1, keepdims=True) + 1e-05)
        return norm_back(centred * rstd, rstd, input_grad[at, :] * gain_row[...])

    @pl.when(step == 3)
    def _():
        for k in range(seg_len // tile):
            context_send[k * tile : (k + 1) * tile, :] = own_rows(k).astype(BF16)
        context_pair.start()

    @pl.when(step == 7)
    def _():
        scatter.tick(16)
        one = jnp.ones((8, 128), F32)
        for acc, row in ((gain_sum, 0), (shift_sum, 2)):
            line = lax.dot_general(
                one,
                acc[...],
                (((1,), (1,)), ((), ())),
                precision=lax.Precision.HIGHEST,
                preferred_element_type=F32,
            )
            small_mine[row : row + 1, :] = line[0:1, 0:LANES]
            small_mine[row + 1 : row + 2, :] = line[0:1, LANES:]

        def to_dp(src, dst, k, index):
            return remote(src, dst, small_send.at[k], small_recv.at[k], index)

        copies = [to_dp(small_mine, small_c.at[1], 0, high * 4 + low * 2 + (1 - core))]
        copies[0].start()
        context_pair.wait_recv()
        for k in range(seg_len // tile):
            at = slice(k * tile, (k + 1) * tile)
            segment_out[0, at] = (
                residual_grad[at, :] + own_rows(k) + context_land[at, :].astype(F32)
            ).astype(BF16)
        copies[0].wait_recv()
        small_c[0] = small_mine[...] + small_c[1]
        copies.append(to_dp(small_c.at[0], small_y.at[1], 1, high * 4 + (1 - low) * 2 + core))
        copies[1].start()
        scatter.tick(17)
        copies[1].wait_recv()
        small_y[0] = small_c[0] + small_y[1]
        along = []
        for k in range(1, nhi):
            to = lax.rem(high + k, nhi) * 4 + low * 2 + core
            along.append(to_dp(small_y.at[0], small_z.at[k], 2 + k, to))
        for copy in along:
            copy.start()
        scatter.tick(18)
        for copy in along:
            copy.wait_recv()
        line = small_y[0]
        for k in range(1, nhi):
            line = line + small_z[k]
        small_z[0] = line
        last = pltpu.make_async_remote_copy(
            src_ref=small_z.at[0],
            dst_ref=small_x,
            send_sem=small_send.at[2],
            recv_sem=small_recv.at[2],
            device_id={"head": 1 - x},
            device_id_type=MESH,
        )
        last.start()
        scatter.tick(19)
        comp_pair.wait_recv()
        to = pl.ds(pl.multiple_of((1 - x) * LANES, LANES), LANES)
        comp_out[:, to] = comp_land[...].astype(F32)
        for f in range(4):
            up_pairs[f].wait_recv()
            up_out[1 - x, f] = up_land[f].astype(F32)
        for b in range(2):
            out_pairs[b].wait_recv()
            out_out[:, b * LANES : (b + 1) * LANES] = out_keep[b] + out_land[b].astype(F32)
        last.wait_recv()
        line = lax.broadcasted_iota(jnp.int32, (SMALL, LANES), 0)
        small_out[...] = small_z[0] + jnp.where(line < 8, small_x[...], 0.0)
        for copy in [context_pair, comp_pair, *up_pairs, *out_pairs, *copies, *along, last]:
            copy.wait_send()
        for c in range(count):
            scatter.close(c)


def attention_backward(
    n, dout, kv, q, wide, near, place_keys, xhat_t, mats, table_t, gain, shift, segment,
    residual_grad, small_in, comp, up, down, out,
):
    _, seg_len, width = segment.shape
    context = kv.shape[2]
    past = context - seg_len
    rows = width // n
    nhi = n // 4
    half_rows = rows // 2
    comp_rows = comp.shape[3] // 2
    const2 = lambda t: (0, 0)
    seq = lambda t: 1 - t // 4
    head = lambda t: lax.rem(t, 4)
    by_both = lambda t: (head(t), seq(t), 0, 0)
    single = pl.Buffered(1)
    any_spec = pl.BlockSpec(memory_space=pl.ANY)
    vmem = pl.BlockSpec(memory_space=pltpu.VMEM)
    dma = pltpu.SemaphoreType.DMA
    f32 = lambda *shape: jax.ShapeDtypeStruct(shape, F32)
    lead = (nhi, 2, 2)
    full = lambda shape: pl.BlockSpec(shape, lambda t: (0,) * len(shape), pipeline_mode=single)
    outs = (
        jax.ShapeDtypeStruct((1, seg_len, width), BF16),
        f32(rows, LANES),
        f32(rows, LANES),
        f32(rows, LANES),
        f32(rows, LANES),
        f32(half_rows, width),
        f32(2, 4, half_rows, LANES),
        f32(2 * rows, width),
        f32(comp_rows, width),
        f32(SMALL, LANES),
    )
    return pl.pallas_call(
        functools.partial(backward_kernel, n, past, seg_len),
        grid=(8,),
        out_shape=outs,
        in_specs=[
            pl.BlockSpec((1, seg_len, 128), lambda t: (seq(t), 0, head(t))),
            pl.BlockSpec((1, 1, context, 256), by_both),
            pl.BlockSpec((1, 1, seg_len, 256), by_both),
            pl.BlockSpec((1, 1, HALF, past + HALF), by_both),
            pl.BlockSpec((1, 1, HALF, seg_len), by_both),
            pl.BlockSpec((1, past + HALF, 128), lambda t: (head(t), 0, 0)),
            pl.BlockSpec((1, width, context), lambda t: (seq(t), 0, 0), pipeline_mode=single),
            *[pl.BlockSpec((width, 128), lambda t: (0, head(t)))] * 3,
            full(table_t.shape),
            full((1, width)),
            full((width, 1)),
            full((width, 1)),
            pl.BlockSpec((1, seg_len, width), lambda t: (seq(t), 0, 0), pipeline_mode=single),
            full((seg_len, width)),
            full((SMALL, LANES)),
            any_spec,
            any_spec,
            any_spec,
            any_spec,
        ],
        out_specs=tuple(full(o.shape) for o in outs),
        scratch_shapes=[
            pltpu.VMEM((width, 384), BF16),
            pltpu.VMEM((4, width, 384), F32),
            pltpu.VMEM((4, 8, 384), F32),
            pltpu.VMEM((4, 128, past + HALF), BF16),
            pltpu.VMEM((seg_len, width), F32),
            pltpu.VMEM((256, context), BF16),
            pltpu.VMEM((width, 128), F32),
            pltpu.VMEM((width, 128), F32),
            pltpu.VMEM((4,) + lead + (rows, LANES), BF16),
            pltpu.VMEM((seg_len, width), BF16),
            pltpu.VMEM((seg_len, width), BF16),
            pltpu.VMEM((4, half_rows, LANES), BF16),
            pltpu.VMEM((4, half_rows, LANES), BF16),
            pltpu.VMEM((3 * rows, LANES), F32),
            pltpu.VMEM((comp_rows, LANES), BF16),
            pltpu.VMEM((comp_rows, LANES), BF16),
            pltpu.VMEM((2, half_rows, LANES), F32),
            pltpu.VMEM((2, half_rows, LANES), BF16),
            pltpu.VMEM((2, half_rows, LANES), BF16),
            pltpu.VMEM((SMALL, LANES), F32),
            pltpu.VMEM((2, SMALL, LANES), F32),
            pltpu.VMEM((2, SMALL, LANES), F32),
            pltpu.VMEM((nhi, SMALL, LANES), F32),
            pltpu.VMEM((SMALL, LANES), F32),
            dma((8,)),
            dma((8,)),
            dma((2 + nhi,)),
            dma((2 + nhi,)),
        ]
        + Scatter.scratch(17, nhi, rows),
        compiler_params=pltpu.CompilerParams(
            vmem_limit_bytes=VMEM_LIMIT,
            dimension_semantics=("arbitrary",),
            collective_id=1,
            has_side_effects=True,
        ),
        name="attention_backward",
    )(
        dout, kv, q, wide, near, place_keys, xhat_t, *mats, table_t,
        gain.reshape(1, width), gain.reshape(width, 1), shift.reshape(width, 1), segment,
        residual_grad, small_in, comp, up, down, out,
    )


def body(
    n,
    segment,
    memory,
    compressed,
    doc_lengths,
    memory_valid,
    query_weight,
    key_weight,
    value_weight,
    position_weight,
    content_bias,
    position_bias,
    output_weight,
    up_weight,
    down_weight,
    compress_weight,
    norm_gain,
    norm_shift,
    post_gain,
    post_shift,
    cotangent,
    compress_cotangent,
):
    x = lax.axis_index("head")
    dp = lax.axis_index("dp")
    first = x == 0
    nhi = n // 4
    width = segment.shape[2]
    seg_len = segment.shape[1]
    past = memory.shape[1] + compressed.shape[1]
    context = past + seg_len
    rows = query_weight.shape[0]
    half_rows = output_weight.shape[0]
    new_count = compress_cotangent.shape[1]
    comp_rows = compress_weight.shape[0]

    def swap(a):
        return lax.ppermute(a, "head", [(0, 1), (1, 0)])

    def pick(a, index):
        return jnp.where(index == 0, a[0], a[1])

    def in_order(own, got, axis):
        return jnp.where(
            first,
            jnp.concatenate([own, got], axis=axis),
            jnp.concatenate([got, own], axis=axis),
        )

    ffr = down_weight.shape[0]
    up_parts = (
        up_weight.reshape(half_rows, 4, n // 4, 2, ffr)
        .transpose(3, 1, 0, 2, 4)
        .reshape(2, 4, half_rows, LANES)
    )
    lane = jnp.arange(width, dtype=jnp.int32)

    def spread(vector, index, size):
        return jnp.where(lane // size == index, jnp.tile(vector, width // size), 0).reshape(2, LANES)

    bias_lane = jnp.arange(LANES, dtype=jnp.int32) % 128
    per = content_bias.shape[1]

    def spread_bias(bias):
        tiled = jnp.tile(bias, (1, n)).reshape(1, LANES)
        return jnp.where((bias_lane // per == dp), tiled, 0)

    small = jnp.concatenate(
        [
            spread(v, dp * 2 + x, half_rows)
            for v in (norm_gain, norm_shift, post_gain, post_shift)
        ]
        + [
            spread_bias(content_bias),
            spread_bias(position_bias),
            jnp.zeros((SMALL - 10, LANES), BF16),
        ]
    ).astype(BF16)

    end_one = doc_lengths[:, 0]
    end_two = end_one + doc_lengths[:, 1]
    docs = jnp.stack([end_one, end_two, end_two + doc_lengths[:, 2], memory_valid], axis=1)
    table = position_rows(context, width, past + HALF)

    (
        att, seg_other, cot_other, params, kv, q, wide, near, place_keys, xhat_t,
        query_whole, key_whole, value_whole, _, out_whole, up_whole, down_whole, comp_whole, *_,
    ) = attention_forward(
        n, docs, compressed, memory, segment, cotangent,
        (query_weight, key_weight, value_weight, position_weight),
        output_weight, up_parts, down_weight, compress_weight, small, jnp.asarray(table),
    )
    mats = [w.reshape(width, LANES) for w in (query_whole, key_whole, value_whole)]
    out_mat = out_whole.reshape(width, width)
    comp_mat = comp_whole.reshape(3 * width, LANES)
    gain_one, shift_one, gain_two, shift_two = (
        params[2 * i : 2 * i + 2].reshape(1, width) for i in range(4)
    )
    segment_both = jnp.concatenate([segment, seg_other[None]])
    cot_both = jnp.concatenate([cotangent[0], cot_other])

    att = att.reshape(-1, width)
    residual, branch, terms, up_grads, down_grads = feed_forward(
        att, segment_both.reshape(-1, width), cot_both, out_mat,
        up_whole.reshape(4, width, LANES), down_whole.reshape(4 * LANES, width), gain_two, shift_two,
    )

    input_terms = terms[:seg_len].astype(F32) + swap(terms[seg_len:]).astype(F32)
    result = (
        residual + branch[:seg_len].astype(F32) + swap(branch[seg_len:]).astype(F32)
    ).astype(BF16)
    mean = jnp.mean(residual, axis=-1, keepdims=True)
    centred = residual - mean
    rstd = lax.rsqrt(jnp.mean(centred * centred, axis=-1, keepdims=True) + 1e-05)
    xhat_two = centred * rstd
    gain_two_grad = jnp.sum(input_terms * xhat_two, axis=0)
    shift_two_grad = jnp.sum(input_terms, axis=0)
    residual_grad = cotangent[0].astype(F32) + norm_back(xhat_two, rstd, input_terms * gain_two)
    branch_grad = residual_grad.astype(BF16)
    out_grads = dot_tn(att[:seg_len], branch_grad).astype(BF16)
    mixed_grad = dot_nt(branch_grad, out_mat).astype(BF16)
    mixed_halves = (mixed_grad[:, :LANES], mixed_grad[:, LANES:])
    dout = jnp.stack([pick(mixed_halves, x), swap(pick(mixed_halves, 1 - x))])

    comp_cot = in_order(compress_cotangent, swap(compress_cotangent), 0)
    windows = memory[:, : 3 * new_count].reshape(-1, 3 * width)
    made_half = dot(windows, comp_mat).astype(BF16).reshape(2, new_count, LANES)
    made = in_order(pick(made_half, x), swap(pick(made_half, 1 - x)), 1)
    comp_cot_half = pick(comp_cot.reshape(-1, 2, LANES).transpose(1, 0, 2), x)
    comp_grads = dot_tn(windows, comp_cot_half).astype(BF16)

    small_in = jnp.concatenate(
        [
            jnp.zeros((4, LANES), F32),
            gain_two_grad.reshape(2, LANES),
            shift_two_grad.reshape(2, LANES),
            jnp.zeros((SMALL - 8, LANES), F32),
        ]
    )
    lead = (nhi, 2, 2)
    (
        segment_grad, query_done, key_done, value_done, place_done,
        out_done, up_done, down_done, comp_done, small_done,
    ) = attention_backward(
        n, dout, kv, q, wide, near, place_keys, xhat_t, mats, jnp.asarray(table.T.copy()),
        gain_one, shift_one, segment_both, residual_grad, small_in,
        comp_grads.reshape(lead + (3 * rows, LANES)),
        up_grads.reshape((4,) + lead + (rows, LANES)),
        down_grads.reshape(lead + (2 * rows, 2 * LANES)),
        out_grads.reshape(lead + (rows, 2 * LANES)),
    )

    up_final = (
        up_done.reshape(2, 4, half_rows, n // 4, ffr)
        .transpose(2, 1, 3, 0, 4)
        .reshape(half_rows, -1)
    )
    vectors = lax.dynamic_slice_in_dim(
        small_done[0:8].reshape(4, width), (dp * 2 + x) * half_rows, half_rows, 1
    )
    biases = lax.dynamic_slice_in_dim(small_done[8:10].reshape(2, 4, 128), dp * per, per, 2)
    return (
        result[None],
        made[None],
        segment_grad,
        query_done,
        key_done,
        value_done,
        place_done,
        biases[0],
        biases[1],
        out_done,
        up_final,
        down_done,
        comp_done,
        vectors[0],
        vectors[1],
        vectors[2],
        vectors[3],
    )


def solution(mesh):
    split = P(("dp", "head"))
    wide = P(("dp", "head"), None)
    deep = P(("dp", "head"), None, None)
    return jax.shard_map(
        functools.partial(body, mesh.shape["dp"]),
        mesh=mesh,
        in_specs=(
            deep,
            P("dp", None, None),
            P("dp", None, None),
            P("dp", None),
            P("dp"),
            P("dp", "head"),
            P("dp", "head"),
            P("dp", "head"),
            P("dp", "head"),
            P("head", "dp"),
            P("head", "dp"),
            wide,
            wide,
            wide,
            wide,
            split,
            split,
            split,
            split,
            deep,
            deep,
        ),
        out_specs=(
            deep,
            deep,
            deep,
            P("dp", "head"),
            P("dp", "head"),
            P("dp", "head"),
            P("dp", "head"),
            P("head", "dp"),
            P("head", "dp"),
            wide,
            wide,
            wide,
            wide,
            split,
            split,
            split,
            split,
        ),
        check_vma=False,
    )
```

time: 2640 us -> 458 us (0.17)
  waiting for transfers between devices: 1220 us -> 51.9 us
  local copies, waits for them, and re-layouts: 716 us -> 37.1 us
  matrix products: 354 us -> 13 us
  Pallas kernels: 0 us -> 320 us
  blocking collectives: 155 us -> 0 us
  other arithmetic: 129 us -> 21.9 us
    reduce_scatter x9 -> x0, waiting for transfers between devices: 1130 us -> none  [the longest x1 361 us: body(): lax.psum_scatter(down_grad, ('dp', 'head'), scatter_dimension=0, tiled=True)]
    while x194 -> x0, local copies, waits for them, and re-layouts: 413 us -> none
    pallas_call x0 -> x3, Pallas kernels: none -> 320 us  [the longest x1 149 us: attention_forward(): pl.pallas_call(functools.partial(forward_kernel, n, past, seg_len), grid=...]
    dot_general x48 -> x4, matrix products: 320 us -> 13 us  [the longest x2 7.75 us: dot_tn(): lax.dot_general(a, b, (((0,), (0,)), ((), ())), preferred_element_type=F32)]
    unnamed x3 -> x0, blocking collectives: 115 us -> none
    reshape x6 -> x10, local copies, waits for them, and re-layouts: 120 us -> 6.82 us  [the longest x1 2.37 us: body(): windows = memory[:, :3 * new_count].reshape(-1, 3 * width)]
    all_gather x9 -> x0, waiting for transfers between devices: 55.2 us -> none  [the longest x1 33.4 us: body(): row_pairs = lax.all_gather(segment, 'head', axis=0, tiled=True)]
    ppermute x0 -> x5, waiting for transfers between devices: none -> 51.9 us  [swap(): return lax.ppermute(a, 'head', [(0, 1), (1, 0)])]
  transfers between devices with their start and end apart: 20 -> 5, of which waited for: 12 -> 2; matrix products, arithmetic and copies ran while one was open for 43% -> 8% of each run, Pallas kernels for 0% -> 0%
where the time goes in v1:
time: 458 us; the launch traced here: 451 us
  Pallas kernels  320 us (70%)
  waiting for transfers between devices  51.9 us (11%)
  local copies, waits for them, and re-layouts  37.1 us (8%)
  other arithmetic  21.9 us (5%)
  matrix products  13 us (3%)
  starting transfers between devices  4.92 us (1%)
    pallas_call x1, Pallas kernels, attention_forward(): pl.pallas_call(functools.partial(forward_kernel, n, past, seg_len), grid=...  149 us
    pallas_call x1, Pallas kernels, attention_backward(): pl.pallas_call(functools.partial(backward_kernel, n, past, seg_len), grid...  127 us
    ppermute x5, waiting for transfers between devices, swap(): return lax.ppermute(a, 'head', [(0, 1), (1, 0)])  51.9 us
    pallas_call x1, Pallas kernels, feed_forward(): pl.pallas_call(feed_kernel, grid=(4,), out_shape=(jax.ShapeDtypeStruct((t...  44.2 us
    unnamed x50, local copies, waits for them, and re-layouts  9.99 us
  transfers between devices with their start and end apart: 5, of which 2 were waited for; matrix products, arithmetic and copies ran while one was open for 8% of the time, Pallas kernels for 0%

profile of v1, /device:TPU:0, one launch (start us, length us, event | category | flops | bytes accessed | tf_op | source)
XLA Modules:
  0.0 450.5 jit_solution(11302020919679121349)
XLA Ops:
  6.8 1.1 reshape.348
  9.5 1.2 concatenate.42.small
  10.8 149.1 %attention_forward.1 = (bf16[2,512,1024]{2,1,0:T(8,128)(2,1)}, bf16[512,1024]{1,0:T(8,128)(2,1)}, bf16[512,1024]{1,0:T(8,128)(2,1)}, f32[16,512]{1,0:T(8,128)}, ...) custom-call(s32[2,4]{1,0:T(2,128)} %pad_add_fusion.docs, ...), custom_call_target="tpu_custom_call" | custom-call | tf_op jit(solution)/shard_map/attention_forward/pallas_call | solution.py:649
  159.9 0.9 slice_bitcast_fusion
  162.0 3.3 pad_maximum_fusion.segment
  165.2 1.6 pad_maximum_fusion.1.cot
  166.8 44.2 %feed_forward.1 = (f32[512,1024]{1,0:T(8,128)}, bf16[1024,1024]{1,0:T(8,128)(2,1)}, bf16[1024,1024]{1,0:T(8,128)(2,1)}, bf16[4,1024,512]{2,1,0:T(8,128)(2,1)}, bf16[2048,1024]{1,0:T(8,128)(2,1)}) custom-call(bf16[1024,1024]{1,0:T(8,128)(2,1)} %bitcast.96, bf16[1024,1024]{1,0:T(8,128)(2,1)} %bitcast.83, bf16[1024,1024]{1,0:T(8,128)(2,1)} %pad_maximum_fusion.1.cot, ...), custom_call_target="tpu_custom_call" | custom-call | tf_op jit(solution)/shard_map/feed_forward/pallas_call | solution.py:809
  211.0 2.4 slice.99
  214.2 1.0 slice.94
  215.2 1.3 collective-permute-start
  217.2 2.4 reshape.358
  219.6 3.9 fusion.4
  223.6 1.4 collective-permute-start.1
  225.6 1.0 copy.62
  226.7 1.0 copy.64
  227.7 44.1 %collective-permute-done.1 = bf16[170,512]{1,0:T(8,128)(2,1)} collective-permute-done((bf16[170,512]{1,0:T(8,128)(2,1)S(1)}, bf16[170,512]{1,0:T(8,128)(2,1)}, u32[]{:S(2)}, u32[]{:S(2)}) %collective-permute-start.1) | collective-permute-done | bytes 174112 | tf_op jit(solution)/shard_map/ppermute | solution.py:1356
  271.8 1.8 maximum_select_fusion.1
  273.6 2.4 maximum_select_fusion
  276.0 2.4 select_n.181
  278.4 2.6 broadcast_select_fusion
  281.0 5.1 %fusion = bf16[3072,512]{0,1:T(8,128)(2,1)} fusion(bf16[340,3072]{1,0:T(8,128)(2,1)} %reshape.358, bf16[1,340,512]{2,0,1:T(2,128)(2,1)S(1)} %broadcast_select_fusion), kind=kOutput, calls=%fused_computation.1 | convolution fusion | flops 1071120384 | bytes 5582848 | tf_op jit(solution)/shard_map/dot_general | solution.py:30
  286.1 4.6 %copy.52 = bf16[3072,512]{1,0:T(8,128)(2,1)} copy(bf16[3072,512]{0,1:T(8,128)(2,1)} %fusion) | data formatting | bytes 6291456 | tf_op jit(solution)/shard_map/convert_element_type | solution.py:1448
  290.8 2.6 multiply_reduce_fusion
  293.4 3.7 multiply_add_fusion
  297.1 1.3 convolution_convert_fusion.2
  300.0 2.6 convolution_convert_fusion.1
  302.6 7.8 %collective-permute-done.3 = bf16[512,512]{1,0:T(8,128)(2,1)S(1)} collective-permute-done((bf16[512,512]{1,0:T(8,128)(2,1)S(1)}, bf16[512,512]{1,0:T(8,128)(2,1)S(1)}, u32[]{:S(2)}, u32[]{:S(2)}) %collective-permute-start.3) | collective-permute-done | bytes 524320 | tf_op jit(solution)/shard_map/ppermute | solution.py:1356
  310.4 1.1 pad_maximum_fusion.2.dout
  311.5 127.0 %attention_backward.1 = (bf16[1,512,1024]{2,1,0:T(8,128)(2,1)}, f32[64,512]{1,0:T(8,128)}, f32[64,512]{1,0:T(8,128)}, f32[64,512]{1,0:T(8,128)}, f32[64,512]{1,0...) custom-call(bf16[2,512,512]{2,1,0:T(8,128)(2,1)} %pad_maximum_fusion, ...), custom_call_target="tpu_custom_call" | custom-call | tf_op jit(solution)/shard_map/attention_backward/pallas_call | solution.py:1247
  440.1 1.2 reshape.370
  441.8 1.2 reshape.371
  444.3 1.0 copy.79
  (96 shorter events, 20.8 us)
Async XLA Ops:
  162.0 3.3 copy-start.1
  162.0 3.3 copy-start.8
  211.0 3.2 copy-start.4
  211.0 6.2 %copy-start.2 = (bf16[2,512,1024]{2,1,0:T(8,128)(2,1)S(1)}, bf16[2,512,1024]{2,1,0:T(8,128)(2,1)}, u32[]{:S(2)}) copy-start(bf16[2,512,1024]{2,1,0:T(8,128)(2,1)} %memory.1) | copy-start | bytes 6291460
  213.4 77.4 %collective-permute-start.2 = (bf16[512,1024]{1,0:T(8,128)(2,1)}, bf16[512,1024]{1,0:T(8,128)(2,1)}, u32[]{:S(2)}, u32[]{:S(2)}) collective-permute-start(bf16[512,1024]{1,0:T(8,128)(2,1)} %slice.99), channel_id=1, source_target_pairs={{0,1},{1,0},{2,3},{3,2},{4,5},{5,4},{6,7},{7,6},{8,9},{9,8},{10,11... | collective-permute-start | bytes 3145736 | tf_op jit(solution)/shard_map/ppermute | solution.py:1356
  215.2 78.2 %collective-permute-start = (bf16[512,1024]{1,0:T(8,128)(2,1)}, bf16[512,1024]{1,0:T(8,128)(2,1)}, u32[]{:S(2)}, u32[]{:S(2)}) collective-permute-start(bf16[512,1024]{1,0:T(8,128)(2,1)} %slice.94), channel_id=1, source_target_pairs={{0,1},{1,0},{2,3},{3,2},{4,5},{5,4},{6,7},{7,6},{8,9},{9,8},{10,11... | collective-permute-start | bytes 3145736 | tf_op jit(solution)/shard_map/ppermute | solution.py:1356
  216.5 57.1 %collective-permute-start.4 = (bf16[1,170,1024]{2,1,0:T(8,128)(2,1)}, bf16[1,170,1024]{2,1,0:T(8,128)(2,1)}, u32[]{:S(2)}, u32[]{:S(2)}) collective-permute-start(bf16[1,170,1024]{2,1,0:T(8,128)(2,1)} %param.43), channel_id=1, source_target_pairs={{0,1},{1,0},{2,3},{3,2},{4,5},{5,4},{6,7},{7,6},{8,9},{9,8},{10,11... | collective-permute-start | bytes 1044488 | tf_op jit(solution)/shard_map/ppermute | solution.py:1356
  219.6 5.4 %copy-start = (f32[512,1024]{1,0:T(8,128)S(1)}, f32[512,1024]{1,0:T(8,128)}, u32[]{:S(2)}) copy-start(f32[512,1024]{1,0:T(8,128)} %get-tuple-element.56) | copy-start | bytes 6291460
  223.6 48.2 %collective-permute-start.1 = (bf16[170,512]{1,0:T(8,128)(2,1)S(1)}, bf16[170,512]{1,0:T(8,128)(2,1)}, u32[]{:S(2)}, u32[]{:S(2)}) collective-permute-start(bf16[170,512]{1,0:T(8,128)(2,1)S(1)} %get-tuple-element.92), channel_id=1, source_target_pairs={{0,1},{1,0},{2,3},{3,2},{4,5},{5,4},{6,7},{7,6},{8,9},{9,8},{10,11... | collective-permute-start | bytes 522248 | tf_op jit(solution)/shard_map/ppermute | solution.py:1356
  225.6 52.8 %copy-start.16 = (f32[1,1,2,512]{3,1,2,0:T(1,128)}, f32[1,1,2,512]{3,1,2,0:T(1,128)S(1)}, u32[]{:S(2)}) copy-start(f32[1,1,2,512]{3,1,2,0:T(1,128)S(1)} %copy.60) | copy-start | bytes 12292
  293.4 3.7 copy-start.6
  297.1 2.9 copy-start.3
  298.4 1.6 copy-start.5
  298.5 11.9 %collective-permute-start.3 = (bf16[512,512]{1,0:T(8,128)(2,1)S(1)}, bf16[512,512]{1,0:T(8,128)(2,1)S(1)}, u32[]{:S(2)}, u32[]{:S(2)}) collective-permute-start(bf16[512,512]{1,0:T(8,128)(2,1)S(1)} %get-tuple-element.90), channel_id=1, source_target_pairs={{0,1},{1,0},{2,3},{3,2},{4,5},{5,4},{6,7},{7,6},{8,9},{9,8},{10,11... | collective-permute-start | bytes 1572872 | tf_op jit(solution)/shard_map/ppermute | solution.py:1356
  438.5 5.7 %copy-start.7 = (bf16[1,512,1024]{2,1,0:T(8,128)(2,1)S(1)}, bf16[1,512,1024]{2,1,0:T(8,128)(2,1)}, u32[]{:S(2)}) copy-start(bf16[1,512,1024]{2,1,0:T(8,128)(2,1)} %get-tuple-element.130) | copy-start | bytes 3145732
  441.3 4.0 copy-start.15
  441.3 4.6 %copy-start.14 = (f32[64,512]{1,0:T(8,128)S(1)}, f32[64,512]{1,0:T(8,128)}, u32[]{:S(2)}) copy-start(f32[64,512]{1,0:T(8,128)} %get-tuple-element.132) | copy-start | bytes 393220
  441.7 4.8 %copy-start.13 = (f32[64,512]{1,0:T(8,128)S(1)}, f32[64,512]{1,0:T(8,128)}, u32[]{:S(2)}) copy-start(f32[64,512]{1,0:T(8,128)} %get-tuple-element.133) | copy-start | bytes 393220
  441.7 5.5 %copy-start.12 = (f32[64,512]{1,0:T(8,128)S(1)}, f32[64,512]{1,0:T(8,128)}, u32[]{:S(2)}) copy-start(f32[64,512]{1,0:T(8,128)} %get-tuple-element.134) | copy-start | bytes 393220
  441.7 6.1 %copy-start.11 = (f32[32,1024]{1,0:T(8,128)S(1)}, f32[32,1024]{1,0:T(8,128)}, u32[]{:S(2)}) copy-start(f32[32,1024]{1,0:T(8,128)} %get-tuple-element.137) | copy-start | bytes 393220
  441.7 6.8 %copy-start.9 = (f32[128,1024]{1,0:T(8,128)S(1)}, f32[128,1024]{1,0:T(8,128)}, u32[]{:S(2)}) copy-start(f32[128,1024]{1,0:T(8,128)} %get-tuple-element.139) | copy-start | bytes 1572868
  444.3 5.1 %copy-start.10 = (f32[96,1024]{1,0:T(8,128)S(1)}, f32[96,1024]{1,0:T(8,128)}, u32[]{:S(2)}) copy-start(f32[96,1024]{1,0:T(8,128)} %get-tuple-element.140) | copy-start | bytes 1179652

commit v2 on v1

--- a/solution.py
+++ b/solution.py
@@ -719,24 +719,37 @@
     square = v * v
     t = jnp.tanh(c * (v + 0.044715 * square * v))
     half = 0.5 * (1.0 + t)
-    slope = half + 0.5 * v * (1.0 - t * t) * (c * (1.0 + 3 * 0.044715 * square))
-    return v * half, slope
+    value = v * half
+    return value, half + value * (1.0 - half) * (2 * c + (6 * 0.044715 * c) * square)
 
 
 def feed_kernel(
+    n,
+    att_in,
+    segment,
+    seg_other,
+    cotangent,
+    cot_other,
+    out_in,
+    up_in,
+    down_in,
+    params,
+    comp,
+    own_out,
+    branch_out,
+    residual_out,
+    dout,
+    out_grads,
+    down_grads,
+    small_out,
+    comp_out,
+    up_out,
     att,
-    segment,
+    seg,
     cot,
     out_w,
     up,
     down,
-    gain,
-    shift,
-    residual_out,
-    branch_out,
-    terms_out,
-    up_out,
-    down_out,
     residual,
     low,
     low_t,
@@ -744,109 +757,344 @@
     pre,
     branch,
     terms,
+    terms_land,
+    cast,
+    up_grads,
+    mixed,
+    stage,
+    up_send,
+    up_land,
+    comp_stage,
+    comp_send,
+    comp_land,
+    load_sem,
+    store_sem,
+    stage_sem,
+    pair_send,
+    pair_recv,
+    land_c,
+    land_y,
+    land_z,
+    mine,
+    mine_sem,
+    *sems,
 ):
-    f = pl.program_id(0)
+    x = lax.axis_index("head")
+    core, low_y, high, nhi = place(n)
     tile = 256
-    total, width = residual.shape
-
-    @pl.when(f == 0)
-    def _():
-        eye = (
-            lax.broadcasted_iota(jnp.int32, (tile, tile), 0)
-            == lax.broadcasted_iota(jnp.int32, (tile, tile), 1)
-        ).astype(BF16)
-
-        def project(i, carry):
-            at = pl.ds(pl.multiple_of(i * tile, tile), tile)
-            residual[at, :] = segment[at, :].astype(F32) + dot(att[at, :], out_w[...])
-            return carry
-
-        lax.fori_loop(0, total // tile, project, 0)
-        for i in range(total // tile):
-            at = slice(i * tile, (i + 1) * tile)
-            value = (norm_rows(residual[at, :]) * gain[...] + shift[...]).astype(BF16)
-            low[at, :] = value
+    _, seg_len, width = att.shape
+    rows = width // n
+    half_rows = rows // 2
+    comp_rows = comp_send.shape[0]
+
+    def pair(src, dst, k):
+        return pltpu.make_async_remote_copy(
+            src_ref=src,
+            dst_ref=dst,
+            send_sem=pair_send.at[k],
+            recv_sem=pair_recv.at[k],
+            device_id={"head": 1 - x},
+            device_id_type=MESH,
+        )
+
+    terms_pair = pair(cast.at[0], terms_land, 0)
+    mixed_pair = pair(mixed.at[1 - x], dout.at[1], 1)
+    comp_pair = pair(comp_send, comp_land, 2)
+    up_pairs = [pair(up_send.at[f], up_land.at[f], 3 + f) for f in range(4)]
+    scatter = Scatter(
+        n,
+        [
+            (part, here, land_c.at[c], land_y.at[c], land_z.at[c], done)
+            for c, (part, here, done) in enumerate(
+                [
+                    (
+                        comp.at[:, :, :, pl.ds(m * rows, rows)],
+                        False,
+                        comp_block(m, x, rows, comp_stage, comp_out, comp_send, comp_pair),
+                    )
+                    for m in range(3)
+                ]
+                + [
+                    (up_grads.at[f], True, up_block(f, x, up_out, up_send, up_pairs[f]))
+                    for f in range(4)
+                ]
+            )
+        ],
+        mine,
+        mine_sem,
+        sems,
+    )
+
+    def load(src, dst, k):
+        return pltpu.make_async_copy(src, dst, load_sem.at[k])
+
+    loads = {
+        "att1": load(att_in.at[1], att.at[1], 0),
+        "out": load(out_in, out_w, 1),
+        "seg1": load(seg_other, seg.at[1], 2),
+        "cot1": load(cot_other, cot.at[1], 3),
+        "up": load(up_in, up, 4),
+        "down": load(down_in, down, 5),
+        "att0": load(att_in.at[0], att.at[0], 6),
+        "seg0": load(segment.at[0], seg.at[0], 7),
+        "cot0": load(cotangent.at[0], cot.at[0], 8),
+    }
+    for copy in loads.values():
+        copy.start()
+    barrier = pltpu.get_barrier_semaphore()
+    pl.semaphore_signal(barrier, inc=1, device_id={"head": 1 - x}, device_id_type=MESH)
+    meet(core, low_y, high, nhi, 1)
+    scatter.start(0)
+    scatter.start(1)
+
+    eye = (
+        lax.broadcasted_iota(jnp.int32, (tile, tile), 0)
+        == lax.broadcasted_iota(jnp.int32, (tile, tile), 1)
+    ).astype(BF16)
+    gain = jnp.concatenate([params[4:5, :], params[5:6, :]], axis=1)
+    shift = jnp.concatenate([params[6:7, :], params[7:8, :]], axis=1)
+
+    def project(i):
+        for k in range(seg_len // tile):
+            at = slice(k * tile, (k + 1) * tile)
+            whole_at = slice(i * seg_len + k * tile, i * seg_len + (k + 1) * tile)
+            value = seg[i, at].astype(F32) + dot(att[i, at], out_w[...])
+            residual[at, :] = value
+            value = (norm_rows(value) * gain + shift).astype(BF16)
+            low[whole_at, :] = value
             for b in range(width // tile):
-                low_t[b * tile : (b + 1) * tile, at] = dot_nt(
+                low_t[b * tile : (b + 1) * tile, whole_at] = dot_nt(
                     eye, value[:, b * tile : (b + 1) * tile]
                 ).astype(BF16)
-        residual_out[...] = residual[0 : total // 2, :]
+
+    def hidden(i):
+        whole_at = slice(i * seg_len, (i + 1) * seg_len)
         branch[...] = jnp.zeros_like(branch)
         terms[...] = jnp.zeros_like(terms)
 
-    def rows_body(i, carry):
-        at = pl.ds(pl.multiple_of(i * tile, tile), tile)
-        value, slope = gelu_parts(dot(low[at, :], up[0]))
-        value = value.astype(BF16)
-        act[at, :] = value
-        back = dot_nt(cot[at, :], down[...]).astype(BF16).astype(F32)
-        back = (back * slope).astype(BF16)
-        pre[at, :] = back
-        branch[at, :] += dot(value, down[...])
-        terms[at, :] += dot_nt(back, up[0])
-        return carry
-
-    lax.fori_loop(0, total // tile, rows_body, 0)
-
-    for i in range(width // tile):
-        at = slice(i * tile, (i + 1) * tile)
-        up_out[0, at, :] = dot(low_t[at, :], pre[...]).astype(BF16)
-    for i in range(LANES // tile):
-        at = slice(i * tile, (i + 1) * tile)
-        down_out[at, :] = dot_tn(act[:, at], cot[...]).astype(BF16)
-
-    @pl.when(f == pl.num_programs(0) - 1)
-    def _():
-        branch_out[...] = branch[...].astype(BF16)
-        terms_out[...] = terms[...].astype(BF16)
-
-
-def feed_forward(att, segment, cot, out_w, up, down, gain, shift):
-    total, width = segment.shape
-    const2 = lambda f: (0, 0)
-    single = pl.Buffered(1)
-    full = lambda: pl.BlockSpec((total, width), const2, pipeline_mode=single)
+        def one(f, carry):
+            down_at = pl.ds(pl.multiple_of(f * LANES, LANES), LANES)
+            value, slope = gelu_parts(dot(low[whole_at, :], up[f]))
+            value = value.astype(BF16)
+            act[f, whole_at, :] = value
+            back = dot_nt(cot[i], down[down_at, :]).astype(BF16).astype(F32)
+            back = (back * slope).astype(BF16)
+            pre[f, whole_at, :] = back
+            branch[...] += dot(value, down[down_at, :])
+            terms[...] += dot_nt(back, up[f])
+            return carry
+
+        lax.fori_loop(0, 4, one, 0)
+
+    for name in ("att1", "out", "seg1"):
+        loads[name].wait()
+    project(1)
+    scatter.add_core(0)
+    scatter.start(2)
+    for name in ("cot1", "up", "down"):
+        loads[name].wait()
+    hidden(1)
+    cast[0] = terms[...].astype(BF16)
+    terms_pair.start()
+    cast[1] = branch[...].astype(BF16)
+    store_branch = pltpu.make_async_copy(cast.at[1], branch_out, store_sem.at[0])
+    store_branch.start()
+    scatter.add_core(1)
+    scatter.add_y(0)
+    for name in ("att0", "seg0", "cot0"):
+        loads[name].wait()
+    project(0)
+    scatter.add_core(2)
+    scatter.add_y(1)
+    scatter.add_z(0)
+    hidden(0)
+    branch[...] += residual[...]
+    store_own = pltpu.make_async_copy(branch, own_out, store_sem.at[1])
+    store_own.start()
+    scatter.add_y(2)
+    scatter.add_z(1)
+
+    block = tile // (4 * rows)
+
+    def up_grad(f):
+        for k in range(width // tile):
+            grad = dot(low_t[k * tile : (k + 1) * tile, :], pre[f]).astype(BF16)
+            up_grads[f, k * block : (k + 1) * block] = grad.reshape(block, 2, 2, rows, LANES)
+        scatter.start(3 + f)
+
+    up_grad(0)
+    scatter.add_z(2)
+    up_grad(1)
+    scatter.add_core(3)
+    up_grad(2)
+    scatter.add_core(4)
+    scatter.add_y(3)
+    up_grad(3)
+    scatter.add_core(5)
+    scatter.add_y(4)
+    scatter.add_z(3)
+
+    terms_pair.wait_recv()
+    gain_grad = jnp.zeros((1, width), F32)
+    shift_grad = jnp.zeros((1, width), F32)
+    terms_pair.wait_send()
+    for k in range(seg_len // tile):
+        at = slice(k * tile, (k + 1) * tile)
+        grad = terms[at, :] + terms_land[at, :].astype(F32)
+        value = residual[at, :]
+        mean = jnp.mean(value, axis=-1, keepdims=True)
+        centred = value - mean
+        rstd = lax.rsqrt(jnp.mean(centred * centred, axis=-1, keepdims=True) + 1e-05)
+        xhat = centred * rstd
+        gain_grad += jnp.sum(grad * xhat, axis=0, keepdims=True)
+        shift_grad += jnp.sum(grad, axis=0, keepdims=True)
+        grad = cot[0, at].astype(F32) + norm_back(xhat, rstd, grad * gain)
+        residual[at, :] = grad
+        grad = grad.astype(BF16)
+        cast[0, at, :] = grad
+        back = dot_nt(grad, out_w[...]).astype(BF16)
+        mixed[0, at, :] = back[:, 0:LANES]
+        mixed[1, at, :] = back[:, LANES:]
+    mixed_pair.start()
+    store_dout = pltpu.make_async_copy(mixed.at[x], dout.at[0], store_sem.at[2])
+    store_dout.start()
+    store_residual = pltpu.make_async_copy(residual, residual_out, store_sem.at[3])
+    store_residual.start()
+    small_out[...] = jnp.zeros_like(small_out)
+    small_out[4:5, :] = gain_grad[:, 0:LANES]
+    small_out[5:6, :] = gain_grad[:, LANES:]
+    small_out[6:7, :] = shift_grad[:, 0:LANES]
+    small_out[7:8, :] = shift_grad[:, LANES:]
+    scatter.add_core(6)
+    scatter.add_y(5)
+    scatter.add_z(4)
+
+    staged = [None, None]
+    jobs = [(out_grads, k * tile, None, k) for k in range(width // tile)]
+    jobs += [
+        (down_grads, f * LANES + k * tile, f, k) for f in range(4) for k in range(LANES // tile)
+    ]
+    for j, (target, start, f, k) in enumerate(jobs):
+        slot = j % 2
+        at = slice(k * tile, (k + 1) * tile)
+        if f is None:
+            grad = dot_tn(att[0, :, at], cast[0])
+        else:
+            grad = dot_tn(act[f, 0:seg_len, at], cot[0]) + dot_tn(act[f, seg_len:, at], cot[1])
+        if staged[slot] is not None:
+            staged[slot].wait()
+        stage[slot] = grad.astype(BF16)
+        staged[slot] = pltpu.make_async_copy(
+            stage.at[slot], target.at[pl.ds(start, tile)], stage_sem.at[slot]
+        )
+        staged[slot].start()
+        if j == 5:
+            scatter.add_y(6)
+            scatter.add_z(5)
+    scatter.add_z(6)
+    comp_pair.wait_recv()
+    to = pl.ds(pl.multiple_of((1 - x) * LANES, LANES), LANES)
+    comp_out[:, to] = comp_land[...].astype(F32)
+    for f in range(4):
+        up_pairs[f].wait_recv()
+        up_out[1 - x, f] = up_land[f].astype(F32)
+    mixed_pair.wait_recv()
+    for copy in [mixed_pair, comp_pair, *up_pairs]:
+        copy.wait_send()
+    for copy in [*staged, store_branch, store_own, store_dout, store_residual]:
+        copy.wait()
+    for c in range(7):
+        scatter.close(c)
+
+
+def comp_block(m, x, rows, stage, out, send, pair):
+    def done(total):
+        stage[m * rows : (m + 1) * rows, :] = total
+        if m == 2:
+            half = send.shape[0]
+            upper, lower = stage[0:half, :], stage[half:, :]
+            to = pl.ds(pl.multiple_of(x * LANES, LANES), LANES)
+            out[:, to] = jnp.where(x == 0, upper, lower)
+            send[...] = jnp.where(x == 0, lower, upper).astype(BF16)
+            pair.start()
+
+    return done
+
+
+def up_block(f, x, out, send, pair):
+    def done(total):
+        half = send.shape[1]
+        upper, lower = total[0:half], total[half:]
+        out[x, f] = jnp.where(x == 0, upper, lower)
+        send[f] = jnp.where(x == 0, lower, upper).astype(BF16)
+        pair.start()
+
+    return done
+
+
+def feed_forward(n, att, segment, seg_other, cotangent, cot_other, out_w, up, down, params, comp):
+    _, seg_len, width = att.shape
+    rows = width // n
+    half_rows = rows // 2
+    nhi = n // 4
+    comp_rows = comp.shape[3] // 2
+    total = 2 * seg_len
+    any_spec = pl.BlockSpec(memory_space=pl.ANY)
+    vmem = pl.BlockSpec(memory_space=pltpu.VMEM)
+    dma = pltpu.SemaphoreType.DMA
+    f32 = lambda *shape: jax.ShapeDtypeStruct(shape, F32)
+    bf = lambda *shape: jax.ShapeDtypeStruct(shape, BF16)
     return pl.pallas_call(
-        feed_kernel,
-        grid=(4,),
+        functools.partial(feed_kernel, n),
         out_shape=(
-            jax.ShapeDtypeStruct((total // 2, width), F32),
-            jax.ShapeDtypeStruct((total, width), BF16),
-            jax.ShapeDtypeStruct((total, width), BF16),
-            jax.ShapeDtypeStruct((4, width, LANES), BF16),
-            jax.ShapeDtypeStruct((4 * LANES, width), BF16),
+            f32(seg_len, width),
+            bf(seg_len, width),
+            f32(seg_len, width),
+            bf(2, seg_len, LANES),
+            bf(width, width),
+            bf(4 * LANES, width),
+            f32(SMALL, LANES),
+            f32(comp_rows, width),
+            f32(2, 4, half_rows, LANES),
         ),
-        in_specs=[
-            full(),
-            full(),
-            full(),
-            pl.BlockSpec((width, width), const2, pipeline_mode=single),
-            pl.BlockSpec((1, width, LANES), lambda f: (f, 0, 0)),
-            pl.BlockSpec((LANES, width), lambda f: (f, 0)),
-            pl.BlockSpec((1, width), const2),
-            pl.BlockSpec((1, width), const2),
-        ],
-        out_specs=(
-            pl.BlockSpec((total // 2, width), const2, pipeline_mode=single),
-            full(),
-            full(),
-            pl.BlockSpec((1, width, LANES), lambda f: (f, 0, 0)),
-            pl.BlockSpec((LANES, width), lambda f: (f, 0)),
-        ),
+        in_specs=[any_spec] * 8 + [vmem, any_spec],
+        out_specs=(any_spec,) * 6 + (vmem,) * 3,
         scratch_shapes=[
-            pltpu.VMEM((total, width), F32),
+            pltpu.VMEM((2, seg_len, width), BF16),
+            pltpu.VMEM((2, seg_len, width), BF16),
+            pltpu.VMEM((2, seg_len, width), BF16),
+            pltpu.VMEM((width, width), BF16),
+            pltpu.VMEM((4, width, LANES), BF16),
+            pltpu.VMEM((4 * LANES, width), BF16),
+            pltpu.VMEM((seg_len, width), F32),
             pltpu.VMEM((total, width), BF16),
             pltpu.VMEM((width, total), BF16),
-            pltpu.VMEM((total, LANES), BF16),
-            pltpu.VMEM((total, LANES), BF16),
-            pltpu.VMEM((total, width), F32),
-            pltpu.VMEM((total, width), F32),
-        ],
+            pltpu.VMEM((4, total, LANES), BF16),
+            pltpu.VMEM((4, total, LANES), BF16),
+            pltpu.VMEM((seg_len, width), F32),
+            pltpu.VMEM((seg_len, width), F32),
+            pltpu.VMEM((seg_len, width), BF16),
+            pltpu.VMEM((2, seg_len, width), BF16),
+            pltpu.VMEM((4, nhi, 2, 2, rows, LANES), BF16),
+            pltpu.VMEM((2, seg_len, LANES), BF16),
+            pltpu.VMEM((2, 256, width), BF16),
+            pltpu.VMEM((4, half_rows, LANES), BF16),
+            pltpu.VMEM((4, half_rows, LANES), BF16),
+            pltpu.VMEM((3 * rows, LANES), F32),
+            pltpu.VMEM((comp_rows, LANES), BF16),
+            pltpu.VMEM((comp_rows, LANES), BF16),
+            dma((9,)),
+            dma((4,)),
+            dma((2,)),
+            dma((7,)),
+            dma((7,)),
+        ]
+        + Scatter.scratch(7, nhi, rows),
         compiler_params=pltpu.CompilerParams(
-            vmem_limit_bytes=VMEM_LIMIT, dimension_semantics=("arbitrary",)
+            vmem_limit_bytes=VMEM_LIMIT, collective_id=2, has_side_effects=True
         ),
         name="feed_forward",
-    )(att, segment, cot, out_w, up, down, gain, shift)
+    )(att, segment, seg_other, cotangent, cot_other, out_w, up, down, params, comp)
 
 
 def norm_back(xhat, rstd, grad):
@@ -876,19 +1124,18 @@
     segment,
     residual_grad,
     small_in,
-    comp,
-    up,
+    own_sum,
+    branch,
     down,
     out,
+    result_out,
     segment_out,
     query_out,
     key_out,
     value_out,
     place_out,
     out_out,
-    up_out,
     down_out,
-    comp_out,
     small_out,
     flat,
     raw,
@@ -901,11 +1148,9 @@
     head_grads,
     context_land,
     context_send,
-    up_send,
-    up_land,
-    comp_stage,
-    comp_send,
-    comp_land,
+    branch_land,
+    own_rows_sum,
+    own_sem,
     out_keep,
     out_send,
     out_land,
@@ -934,7 +1179,6 @@
     width = flat.shape[0]
     rows = width // n
     half_rows = rows // 2
-    comp_rows = comp_send.shape[0]
     scale = 1.0 / math.sqrt(128)
     flip = (
         lax.broadcasted_iota(jnp.int32, (HALF, HALF), 0)
@@ -953,30 +1197,9 @@
         )
 
     context_pair = pair(context_send, context_land, 0)
-    comp_pair = pair(comp_send, comp_land, 1)
-    up_pairs = [pair(up_send.at[f], up_land.at[f], 2 + f) for f in range(4)]
-    out_pairs = [pair(out_send.at[b], out_land.at[b], 6 + b) for b in range(2)]
-
-    def comp_done(m):
-        def done(total):
-            comp_stage[m * rows : (m + 1) * rows, :] = total
-            if m == 2:
-                upper, lower = comp_stage[0:comp_rows, :], comp_stage[comp_rows:, :]
-                to = pl.ds(pl.multiple_of(x * LANES, LANES), LANES)
-                comp_out[:, to] = jnp.where(x == 0, upper, lower)
-                comp_send[...] = jnp.where(x == 0, lower, upper).astype(BF16)
-                comp_pair.start()
-
-        return done
-
-    def up_done(f):
-        def done(total):
-            upper, lower = total[0:half_rows], total[half_rows:]
-            up_out[x, f] = jnp.where(x == 0, upper, lower)
-            up_send[f] = jnp.where(x == 0, lower, upper).astype(BF16)
-            up_pairs[f].start()
-
-        return done
+    branch_pair = pair(branch, branch_land, 1)
+    out_pairs = [pair(out_send.at[b], out_land.at[b], 2 + b) for b in range(2)]
+    load_own = pltpu.make_async_copy(own_sum, own_rows_sum, own_sem)
 
     def down_done(a, b):
         def done(total):
@@ -1000,10 +1223,7 @@
 
         return done
 
-    parts = [
-        (comp.at[:, :, :, pl.ds(m * rows, rows)], False, comp_done(m)) for m in range(3)
-    ]
-    parts += [(up.at[f], False, up_done(f)) for f in range(4)]
+    parts = []
     for a in range(2):
         for b in range(2):
             at, to = pl.ds(a * rows, rows), pl.ds(b * LANES, LANES)
@@ -1029,6 +1249,7 @@
         barrier = pltpu.get_barrier_semaphore()
         pl.semaphore_signal(barrier, inc=1, device_id={"head": 1 - x}, device_id_type=MESH)
         meet(core, low, high, nhi, 1)
+        load_own.start()
         raw[...] = jnp.zeros_like(raw)
         sums[...] = jnp.zeros_like(sums)
         place_sum[...] = jnp.zeros_like(place_sum)
@@ -1040,8 +1261,11 @@
     def _():
         input_grad[...] = jnp.zeros_like(input_grad)
 
-    for k in range(8):
-        pl.when(step == k)(functools.partial(scatter.tick, 2 * k))
+    before = {0: 0, 1: 2, 2: 4, 3: None, 4: None, 5: 6, 6: 7, 7: 8}
+    within = {0: 1, 1: 3, 2: 5}
+    for k, t in before.items():
+        if t is not None:
+            pl.when(step == k)(functools.partial(scatter.tick, t))
 
     for j, mat in enumerate((query_w, key_w, value_w)):
         flat[:, j * 128 : (j + 1) * 128] = mat[...]
@@ -1093,8 +1317,8 @@
     dq = jnp.concatenate(query_grads, axis=0)
     stacked = jnp.concatenate([dq, dkv[:, past:].astype(F32).T.astype(BF16)], axis=1)
 
-    for k in range(8):
-        pl.when(step == k)(functools.partial(scatter.tick, 2 * k + 1))
+    for k, t in within.items():
+        pl.when(step == k)(functools.partial(scatter.tick, t))
 
     ones = jnp.ones((8, context), BF16)
     sums[head, :, 0:128] += dot(ones[:, 0:seg_len], dq)
@@ -1135,10 +1359,11 @@
         for k in range(seg_len // tile):
             context_send[k * tile : (k + 1) * tile, :] = own_rows(k).astype(BF16)
         context_pair.start()
+        branch_pair.start()
 
     @pl.when(step == 7)
     def _():
-        scatter.tick(16)
+        scatter.tick(9)
         one = jnp.ones((8, 128), F32)
         for acc, row in ((gain_sum, 0), (shift_sum, 2)):
             line = lax.dot_general(
@@ -1166,7 +1391,7 @@
         small_c[0] = small_mine[...] + small_c[1]
         copies.append(to_dp(small_c.at[0], small_y.at[1], 1, high * 4 + (1 - low) * 2 + core))
         copies[1].start()
-        scatter.tick(17)
+        scatter.tick(10)
         copies[1].wait_recv()
         small_y[0] = small_c[0] + small_y[1]
         along = []
@@ -1175,7 +1400,7 @@
             along.append(to_dp(small_y.at[0], small_z.at[k], 2 + k, to))
         for copy in along:
             copy.start()
-        scatter.tick(18)
+        scatter.tick(11)
         for copy in along:
             copy.wait_recv()
         line = small_y[0]
@@ -1191,20 +1416,19 @@
             device_id_type=MESH,
         )
         last.start()
-        scatter.tick(19)
-        comp_pair.wait_recv()
-        to = pl.ds(pl.multiple_of((1 - x) * LANES, LANES), LANES)
-        comp_out[:, to] = comp_land[...].astype(F32)
-        for f in range(4):
-            up_pairs[f].wait_recv()
-            up_out[1 - x, f] = up_land[f].astype(F32)
+        scatter.tick(12)
+        branch_pair.wait_recv()
+        load_own.wait()
+        for k in range(seg_len // tile):
+            at = slice(k * tile, (k + 1) * tile)
+            result_out[0, at] = (own_rows_sum[at, :] + branch_land[at, :].astype(F32)).astype(BF16)
         for b in range(2):
             out_pairs[b].wait_recv()
             out_out[:, b * LANES : (b + 1) * LANES] = out_keep[b] + out_land[b].astype(F32)
         last.wait_recv()
         line = lax.broadcasted_iota(jnp.int32, (SMALL, LANES), 0)
         small_out[...] = small_z[0] + jnp.where(line < 8, small_x[...], 0.0)
-        for copy in [context_pair, comp_pair, *up_pairs, *out_pairs, *copies, *along, last]:
+        for copy in [context_pair, branch_pair, *out_pairs, *copies, *along, last]:
             copy.wait_send()
         for c in range(count):
             scatter.close(c)
@@ -1212,7 +1436,7 @@
 
 def attention_backward(
     n, dout, kv, q, wide, near, place_keys, xhat_t, mats, table_t, gain, shift, segment,
-    residual_grad, small_in, comp, up, down, out,
+    residual_grad, small_in, own_sum, branch, down, out,
 ):
     _, seg_len, width = segment.shape
     context = kv.shape[2]
@@ -1220,28 +1444,24 @@
     rows = width // n
     nhi = n // 4
     half_rows = rows // 2
-    comp_rows = comp.shape[3] // 2
-    const2 = lambda t: (0, 0)
     seq = lambda t: 1 - t // 4
     head = lambda t: lax.rem(t, 4)
     by_both = lambda t: (head(t), seq(t), 0, 0)
     single = pl.Buffered(1)
     any_spec = pl.BlockSpec(memory_space=pl.ANY)
-    vmem = pl.BlockSpec(memory_space=pltpu.VMEM)
     dma = pltpu.SemaphoreType.DMA
     f32 = lambda *shape: jax.ShapeDtypeStruct(shape, F32)
     lead = (nhi, 2, 2)
     full = lambda shape: pl.BlockSpec(shape, lambda t: (0,) * len(shape), pipeline_mode=single)
     outs = (
         jax.ShapeDtypeStruct((1, seg_len, width), BF16),
+        jax.ShapeDtypeStruct((1, seg_len, width), BF16),
         f32(rows, LANES),
         f32(rows, LANES),
         f32(rows, LANES),
         f32(rows, LANES),
         f32(half_rows, width),
-        f32(2, 4, half_rows, LANES),
         f32(2 * rows, width),
-        f32(comp_rows, width),
         f32(SMALL, LANES),
     )
     return pl.pallas_call(
@@ -1282,11 +1502,9 @@
             pltpu.VMEM((4,) + lead + (rows, LANES), BF16),
             pltpu.VMEM((seg_len, width), BF16),
             pltpu.VMEM((seg_len, width), BF16),
-            pltpu.VMEM((4, half_rows, LANES), BF16),
-            pltpu.VMEM((4, half_rows, LANES), BF16),
-            pltpu.VMEM((3 * rows, LANES), F32),
-            pltpu.VMEM((comp_rows, LANES), BF16),
-            pltpu.VMEM((comp_rows, LANES), BF16),
+            pltpu.VMEM((seg_len, width), BF16),
+            pltpu.VMEM((seg_len, width), F32),
+            dma(()),
             pltpu.VMEM((2, half_rows, LANES), F32),
             pltpu.VMEM((2, half_rows, LANES), BF16),
             pltpu.VMEM((2, half_rows, LANES), BF16),
@@ -1295,12 +1513,12 @@
             pltpu.VMEM((2, SMALL, LANES), F32),
             pltpu.VMEM((nhi, SMALL, LANES), F32),
             pltpu.VMEM((SMALL, LANES), F32),
-            dma((8,)),
-            dma((8,)),
+            dma((4,)),
+            dma((4,)),
             dma((2 + nhi,)),
             dma((2 + nhi,)),
         ]
-        + Scatter.scratch(17, nhi, rows),
+        + Scatter.scratch(10, nhi, rows),
         compiler_params=pltpu.CompilerParams(
             vmem_limit_bytes=VMEM_LIMIT,
             dimension_semantics=("arbitrary",),
@@ -1311,7 +1529,7 @@
     )(
         dout, kv, q, wide, near, place_keys, xhat_t, *mats, table_t,
         gain.reshape(1, width), gain.reshape(width, 1), shift.reshape(width, 1), segment,
-        residual_grad, small_in, comp, up, down, out,
+        residual_grad, small_in, own_sum, branch, down, out,
     )
 
 
@@ -1411,35 +1629,8 @@
     mats = [w.reshape(width, LANES) for w in (query_whole, key_whole, value_whole)]
     out_mat = out_whole.reshape(width, width)
     comp_mat = comp_whole.reshape(3 * width, LANES)
-    gain_one, shift_one, gain_two, shift_two = (
-        params[2 * i : 2 * i + 2].reshape(1, width) for i in range(4)
-    )
+    gain_one, shift_one = (params[2 * i : 2 * i + 2].reshape(1, width) for i in range(2))
     segment_both = jnp.concatenate([segment, seg_other[None]])
-    cot_both = jnp.concatenate([cotangent[0], cot_other])
-
-    att = att.reshape(-1, width)
-    residual, branch, terms, up_grads, down_grads = feed_forward(
-        att, segment_both.reshape(-1, width), cot_both, out_mat,
-        up_whole.reshape(4, width, LANES), down_whole.reshape(4 * LANES, width), gain_two, shift_two,
-    )
-
-    input_terms = terms[:seg_len].astype(F32) + swap(terms[seg_len:]).astype(F32)
-    result = (
-        residual + branch[:seg_len].astype(F32) + swap(branch[seg_len:]).astype(F32)
-    ).astype(BF16)
-    mean = jnp.mean(residual, axis=-1, keepdims=True)
-    centred = residual - mean
-    rstd = lax.rsqrt(jnp.mean(centred * centred, axis=-1, keepdims=True) + 1e-05)
-    xhat_two = centred * rstd
-    gain_two_grad = jnp.sum(input_terms * xhat_two, axis=0)
-    shift_two_grad = jnp.sum(input_terms, axis=0)
-    residual_grad = cotangent[0].astype(F32) + norm_back(xhat_two, rstd, input_terms * gain_two)
-    branch_grad = residual_grad.astype(BF16)
-    out_grads = dot_tn(att[:seg_len], branch_grad).astype(BF16)
-    mixed_grad = dot_nt(branch_grad, out_mat).astype(BF16)
-    mixed_halves = (mixed_grad[:, :LANES], mixed_grad[:, LANES:])
-    dout = jnp.stack([pick(mixed_halves, x), swap(pick(mixed_halves, 1 - x))])
-
     comp_cot = in_order(compress_cotangent, swap(compress_cotangent), 0)
     windows = memory[:, : 3 * new_count].reshape(-1, 3 * width)
     made_half = dot(windows, comp_mat).astype(BF16).reshape(2, new_count, LANES)
@@ -1447,23 +1638,19 @@
     comp_cot_half = pick(comp_cot.reshape(-1, 2, LANES).transpose(1, 0, 2), x)
     comp_grads = dot_tn(windows, comp_cot_half).astype(BF16)
 
-    small_in = jnp.concatenate(
-        [
-            jnp.zeros((4, LANES), F32),
-            gain_two_grad.reshape(2, LANES),
-            shift_two_grad.reshape(2, LANES),
-            jnp.zeros((SMALL - 8, LANES), F32),
-        ]
+    lead = (nhi, 2, 2)
+    own_sum, branch, residual_grad, dout, out_grads, down_grads, small_in, comp_done, up_done = feed_forward(
+        n, att, segment, seg_other, cotangent, cot_other, out_mat,
+        up_whole.reshape(4, width, LANES), down_whole.reshape(4 * LANES, width), params,
+        comp_grads.reshape(lead + (3 * rows, LANES)),
     )
-    lead = (nhi, 2, 2)
+
     (
-        segment_grad, query_done, key_done, value_done, place_done,
-        out_done, up_done, down_done, comp_done, small_done,
+        result, segment_grad, query_done, key_done, value_done, place_done,
+        out_done, down_done, small_done,
     ) = attention_backward(
         n, dout, kv, q, wide, near, place_keys, xhat_t, mats, jnp.asarray(table.T.copy()),
-        gain_one, shift_one, segment_both, residual_grad, small_in,
-        comp_grads.reshape(lead + (3 * rows, LANES)),
-        up_grads.reshape((4,) + lead + (rows, LANES)),
+        gain_one, shift_one, segment_both, residual_grad, small_in, own_sum, branch,
         down_grads.reshape(lead + (2 * rows, 2 * LANES)),
         out_grads.reshape(lead + (rows, 2 * LANES)),
     )
@@ -1478,7 +1665,7 @@
     )
     biases = lax.dynamic_slice_in_dim(small_done[8:10].reshape(2, 4, 128), dp * per, per, 2)
     return (
-        result[None],
+        result,
         made[None],
         segment_grad,
         query_done,

time: 458 us -> 395 us (0.86)
  waiting for transfers between devices: 51.9 us -> 0.01 us
  Pallas kernels: 320 us -> 339 us
  other arithmetic: 21.9 us -> 5.25 us
  local copies, waits for them, and re-layouts: 37.1 us -> 30 us
  matrix products: 13 us -> 7.36 us
    ppermute x5 -> x2, waiting for transfers between devices: 51.9 us -> 0.01 us  [swap(): return lax.ppermute(a, 'head', [(0, 1), (1, 0)])]
    pallas_call x1, Pallas kernels: 44.2 us -> 92.3 us  [feed_forward(): pl.pallas_call(functools.partial(feed_kernel, n), out_shape=(f32(seg_len,...]
    pallas_call x1, Pallas kernels: 127 us -> 100 us  [attention_backward(): pl.pallas_call(functools.partial(backward_kernel, n, past, seg_len), grid...]
    unnamed x50 -> x42, local copies, waits for them, and re-layouts: 9.99 us -> 9.68 us
  transfers between devices with their start and end apart: 5 -> 2, of which waited for: 2 -> 0; matrix products, arithmetic and copies ran while one was open for 8% -> 6% of each run, Pallas kernels for 0% -> 38%
where the time goes in v2:
time: 395 us; the launch traced here: 388 us
  Pallas kernels  339 us (86%)
  local copies, waits for them, and re-layouts  30 us (8%)
  matrix products  7.36 us (2%)
  other arithmetic  5.25 us (1%)
  starting transfers between devices  4.36 us (1%)
    pallas_call x1, Pallas kernels, attention_forward(): pl.pallas_call(functools.partial(forward_kernel, n, past, seg_len), grid=...  147 us
    pallas_call x1, Pallas kernels, attention_backward(): pl.pallas_call(functools.partial(backward_kernel, n, past, seg_len), grid...  100 us
    pallas_call x1, Pallas kernels, feed_forward(): pl.pallas_call(functools.partial(feed_kernel, n), out_shape=(f32(seg_len,...  92.3 us
    unnamed x42, local copies, waits for them, and re-layouts  9.68 us
  transfers between devices with their start and end apart: 2, of which 0 were waited for; matrix products, arithmetic and copies ran while one was open for 6% of the time, Pallas kernels for 38%

profile of v2, /device:TPU:0, one launch (start us, length us, event | category | flops | bytes accessed | tf_op | source)
XLA Modules:
  0.0 387.7 jit_solution(10457618125860199174)
XLA Ops:
  0.7 3.0 collective-permute-start
  3.7 0.7 copy.50
  4.4 0.9 slice_add_fusion
  5.3 0.7 tile.60
  6.0 0.7 tile.63
  7.5 0.7 tile.69
  8.2 0.7 tile.72
  9.0 0.7 tile.74
  9.8 1.1 reshape.305
  11.0 0.8 reshape.306.up_parts
  11.8 4.0 %reshape.310 = bf16[340,3072]{1,0:T(8,128)(2,1)} reshape(bf16[2,510,1024]{2,1,0:T(8,128)(2,1)} %bitcast.59) | data formatting | bytes 4177920 | tf_op jit(solution)/shard_map/reshape | solution.py:1635
  16.5 1.2 concatenate.36.small
  17.8 146.9 %attention_forward.1 = (bf16[2,512,1024]{2,1,0:T(8,128)(2,1)}, bf16[512,1024]{1,0:T(8,128)(2,1)}, bf16[512,1024]{1,0:T(8,128)(2,1)}, f32[16,512]{1,0:T(8,128)}, ...) custom-call(s32[2,4]{1,0:T(2,128)} %pad_add_fusion.docs, ...), custom_call_target="tpu_custom_call" | custom-call | tf_op jit(solution)/shard_map/attention_forward/pallas_call | solution.py:649
  164.7 3.9 %fusion.1 = bf16[340,512]{1,0:T(8,128)(2,1)S(1)} fusion(bf16[3072,512]{1,0:T(8,128)(2,1)} %bitcast.78, bf16[340,3072]{1,0:T(8,128)(2,1)} %reshape.310), kind=kOutput, calls=%fused_computation.5 | convolution fusion | flops 1069721600 | bytes 5582848 | tf_op jit(solution)/shard_map/dot_general | solution.py:22
  168.6 1.4 collective-permute-start.1
  170.0 0.8 slice_bitcast_fusion
  170.8 1.0 copy.61
  171.9 1.0 copy.59
  172.9 1.5 pad_maximum_fusion.segment
  174.4 0.8 maximum_select_fusion.1
  175.8 1.2 broadcast_select_fusion
  176.9 3.5 fusion
  180.4 2.8 copy.52
  183.3 92.3 %feed_forward.1 = (f32[512,1024]{1,0:T(8,128)}, bf16[512,1024]{1,0:T(8,128)(2,1)}, f32[512,1024]{1,0:T(8,128)}, bf16[2,512,512]{2,1,0:T(8,128)(2,1)}, bf16[1024,...) custom-call(bf16[2,512,1024]{2,1,0:T(8,128)(2,1)} %get-tuple-element, ...), custom_call_target="tpu_custom_call" | custom-call | tf_op jit(solution)/shard_map/feed_forward/pallas_call | solution.py:1047
  275.6 100.2 %attention_backward.1 = (bf16[1,512,1024]{2,1,0:T(8,128)(2,1)}, bf16[1,512,1024]{2,1,0:T(8,128)(2,1)}, f32[64,512]{1,0:T(8,128)}, f32[64,512]{1,0:T(8,128)}, f32...) custom-call(bf16[2,512,512]{2,1,0:T(8,128)(2,1)} %get-tuple-element.59., ...), custom_call_target="tpu_custom_call" | custom-call | tf_op jit(solution)/shard_map/attention_backward/pallas_call | solution.py:1467
  375.8 0.8 slice.68
  376.6 0.7 slice.71
  378.0 1.2 reshape.321
  380.5 1.0 copy.77
  381.5 1.0 copy.78
  385.7 0.8 copy.84
  386.5 0.7 copy.85
  (60 shorter events, 7.8 us)
Async XLA Ops:
  0.7 174.6 %collective-permute-start = (bf16[1,170,1024]{2,1,0:T(8,128)(2,1)}, bf16[1,170,1024]{2,1,0:T(8,128)(2,1)S(1)}, u32[]{:S(2)}, u32[]{:S(2)}) collective-permute-start(bf16[1,170,1024]{2,1,0:T(8,128)(2,1)} %param.43), channel_id=1, source_target_pairs={{0,1},{1,0},{2,3},{3,2},{4,5},{5,4},{6,7},{7,6},{8,9},{9,8},{10,11... | collective-permute-start | bytes 1044488 | tf_op jit(solution)/shard_map/ppermute | solution.py:1574
  164.7 8.2 %copy-start.1 = (bf16[512,1024]{1,0:T(8,128)(2,1)S(1)}, bf16[512,1024]{1,0:T(8,128)(2,1)}, u32[]{:S(2)}) copy-start(bf16[512,1024]{1,0:T(8,128)(2,1)} %get-tuple-element.53.seg_other) | copy-start | bytes 3145732
  168.6 4.3 %copy-start = (bf16[1,512,1024]{2,1,0:T(8,128)(2,1)S(1)}, bf16[1,512,1024]{2,1,0:T(8,128)(2,1)}, u32[]{:S(2)}) copy-start(bf16[1,512,1024]{2,1,0:T(8,128)(2,1)} %segment.3) | copy-start | bytes 3145732
  168.6 5.8 %collective-permute-start.1 = (bf16[170,512]{1,0:T(8,128)(2,1)S(1)}, bf16[170,512]{1,0:T(8,128)(2,1)S(1)}, u32[]{:S(2)}, u32[]{:S(2)}) collective-permute-start(bf16[170,512]{1,0:T(8,128)(2,1)S(1)} %get-tuple-element.90), channel_id=1, source_target_pairs={{0,1},{1,0},{2,3},{3,2},{4,5},{5,4},{6,7},{7,6},{8,9},{9,8},{10,11... | collective-permute-start | bytes 522248 | tf_op jit(solution)/shard_map/ppermute | solution.py:1574
  170.8 3.6 copy-start.13
  172.9 2.3 copy-start.7
  275.6 101.8 %copy-start.5 = (f32[2,4,32,512]{3,2,1,0:T(8,128)S(1)}, f32[2,4,32,512]{3,2,1,0:T(8,128)}, u32[]{:S(2)}) copy-start(f32[2,4,32,512]{3,2,1,0:T(8,128)} %get-tuple-element.84) | copy-start | bytes 1572868
  375.8 4.7 %copy-start.3 = (bf16[1,512,1024]{2,1,0:T(8,128)(2,1)S(1)}, bf16[1,512,1024]{2,1,0:T(8,128)(2,1)}, u32[]{:S(2)}) copy-start(bf16[1,512,1024]{2,1,0:T(8,128)(2,1)} %get-tuple-element.123) | copy-start | bytes 3145732
  377.5 3.9 %copy-start.2 = (bf16[1,512,1024]{2,1,0:T(8,128)(2,1)S(1)}, bf16[1,512,1024]{2,1,0:T(8,128)(2,1)}, u32[]{:S(2)}) copy-start(bf16[1,512,1024]{2,1,0:T(8,128)(2,1)} %get-tuple-element.125) | copy-start | bytes 3145732
  379.8 2.6 copy-start.12
  380.5 2.6 copy-start.11
  380.5 3.3 copy-start.10
  380.5 3.9 %copy-start.9 = (f32[64,512]{1,0:T(8,128)S(1)}, f32[64,512]{1,0:T(8,128)}, u32[]{:S(2)}) copy-start(f32[64,512]{1,0:T(8,128)} %get-tuple-element.129) | copy-start | bytes 393220
  380.5 4.6 %copy-start.8 = (f32[32,1024]{1,0:T(8,128)S(1)}, f32[32,1024]{1,0:T(8,128)}, u32[]{:S(2)}) copy-start(f32[32,1024]{1,0:T(8,128)} %get-tuple-element.132) | copy-start | bytes 393220
  381.5 4.3 %copy-start.4 = (f32[128,1024]{1,0:T(8,128)S(1)}, f32[128,1024]{1,0:T(8,128)}, u32[]{:S(2)}) copy-start(f32[128,1024]{1,0:T(8,128)} %get-tuple-element.134) | copy-start | bytes 1572868
  381.5 5.1 %copy-start.6 = (f32[96,1024]{1,0:T(8,128)S(1)}, f32[96,1024]{1,0:T(8,128)}, u32[]{:S(2)}) copy-start(f32[96,1024]{1,0:T(8,128)} %get-tuple-element.135) | copy-start | bytes 1179652
